TPU v7x, 32 devices: a whole 2x2x4 slice. The times are simulated.
32 devices in a mesh: groups: 2 (over y), wide: 16 (over z, x, core), narrow: 1.
Axes of the slice: x: 2, y: 2, z: 4, core: 2. Of those that a mesh axis runs over, the one named last changes fastest.
Arguments:
- tokens: bfloat16 [2048, 2560], P(('groups', 'wide'), 'narrow'), parts along dimension 0, may hold values from -6 to 6
- expert_ids: int32 [2048, 2], P(('groups', 'wide')), parts along dimension 0, may hold values from 0 to 7, all different within a row; in each aligned block of 64 rows (0 to 63, 64 to 127, ...) at most 32 rows name the same one
- route_weights: float32 [2048, 2], P(('groups', 'wide')), parts along dimension 0, may hold values from 0.1 to 1
- gate_weight: bfloat16 [16, 384, 2560], P('wide', 'narrow'), may hold values from -0.125 to 0.125
- up_weight: bfloat16 [16, 384, 2560], P('wide', 'narrow'), may hold values from -0.125 to 0.125
- down_weight: bfloat16 [16, 384, 2560], P('wide', 'narrow'), may hold values from -0.21875 to 0.21875
Outputs:
- mixed: bfloat16 [2048, 2560], P(('groups', 'wide'), 'narrow'), parts along dimension 0
There are 2 independent parts, one for each index of `groups`. A program takes and returns all parts, laid end to end along the dimension named above; an argument that names none is the same for every part. Nothing has to cross between parts.
Inputs may be any that keep to these rules, and one draw needn't show every extreme that they name: `expert_ids`: each row names 2 different experts. Within the rows of one device (64 tokens along wide) no expert is named more than 32 times, a bound that some block reaches.
All inputs are finite; a program needn't handle non-finite values.
Results may differ from a plain program's by a relative error of at most 0.0057.
Values may be sent and summed in bfloat16 or wider, within the bound.
A program may use at most 64 MiB of HBM per device.

v0:
```python
import jax
import jax.numpy as jnp
from jax import lax
from jax.sharding import PartitionSpec as P


def per_device(tokens, expert_ids, route_weights, gate_weight, up_weight, down_weight):
    tok_rows = tokens.shape[0]
    picks = expert_ids.shape[1]
    width_wide = lax.axis_size("wide")
    experts = width_wide // 2
    slots = 4 * tok_rows * picks // width_wide
    payload = lax.all_gather(tokens, "narrow", axis=1, tiled=True)
    feature_width = payload.shape[1]
    flat_ids = expert_ids.reshape(-1)
    flat_weights = route_weights.reshape(-1)
    onehot = (flat_ids[:, None] == jnp.arange(experts, dtype=jnp.int32)[None, :]).astype(jnp.int32)
    slot_rank = jnp.sum(jnp.cumsum(onehot, axis=0) * onehot, axis=1) - 1
    slot_place = flat_ids * slots + slot_rank
    token_source = jnp.arange(tok_rows * picks, dtype=jnp.int32) // picks
    slot_token = jnp.full((experts * slots,), tok_rows, jnp.int32).at[slot_place].set(token_source)
    padded = jnp.concatenate([payload, jnp.zeros((1, feature_width), payload.dtype)], axis=0)
    buffer = padded[slot_token].reshape(experts, slots, feature_width)
    outgoing = jnp.repeat(buffer, 2, axis=0)
    received = lax.all_to_all(outgoing, "wide", split_axis=0, concat_axis=0, tiled=True)
    model_width = received.shape[2]
    rows = received.reshape(width_wide * slots, model_width)
    gate = jnp.einsum("rd,hd->rh", rows, gate_weight[0], preferred_element_type=jnp.float32)
    up_part = jnp.einsum("rd,hd->rh", rows, up_weight[0], preferred_element_type=jnp.float32)
    hidden = (jax.nn.silu(gate) * up_part).astype(jnp.bfloat16)
    quarter_out = jnp.dot(hidden, down_weight[0], preferred_element_type=jnp.float32)
    quarter_blocks = quarter_out.reshape(width_wide, slots, model_width)
    returned = lax.all_to_all(quarter_blocks, "wide", split_axis=0, concat_axis=0, tiled=True)
    by_expert = jnp.sum(returned.reshape(experts, 2, slots, model_width), axis=1)
    pieces = by_expert[flat_ids, slot_rank]
    expert_total = lax.psum_scatter(pieces, "narrow", scatter_dimension=1, tiled=True)
    rounded = lax.optimization_barrier(expert_total.astype(jnp.bfloat16))
    pair_total = rounded.astype(jnp.float32) * flat_weights[:, None]
    column_width = pair_total.shape[1]
    mixed = jnp.sum(pair_total.reshape(tok_rows, picks, column_width), axis=1)
    return mixed.astype(jnp.bfloat16)


def solution(mesh):
    in_specs = (
        P(("groups", "wide"), "narrow"),
        P(("groups", "wide"), None),
        P(("groups", "wide"), None),
        P("wide", "narrow", None),
        P("wide", "narrow", None),
        P("wide", "narrow", None),
    )
    out_specs = P(("groups", "wide"), "narrow")
    return jax.shard_map(
        per_device, mesh=mesh, in_specs=in_specs, out_specs=out_specs, check_vma=False
    )
```

profile of v0, /device:TPU:11, one launch (start us, length us, event | category | flops | bytes accessed | tf_op | source)
XLA Modules:
  0.0 213.5 jit_solution(17222675582362970659)
XLA Ops:
  0.0 0.9 copy.10
  0.9 0.1 eq.15
  1.1 0.1 reshape.96
  1.2 0.1 fusion.12
  1.3 0.2 reduce_window_sum.11
  1.5 0.2 select_reduce_fusion
  1.7 1.0 scatter_custom_fusion
  2.7 1.0 concatenate.6
  3.7 2.5 %gather_fusion = bf16[256,2560]{1,0:T(8,128)(2,1)} fusion(bf16[65,2560]{1,0:T(8,128)(2,1)S(1)} %concatenate.6, s32[1024]{0:T(1024)S(1)} %pad_clamp_fusion), kind=kCustom, calls=%fused_computation | custom fusion | bytes 2622464 | tf_op jit(solution)/shard_map/gather | solution.py:23
  6.2 1.6 broadcast_in_dim.16
  7.8 65.0 %all_to_all.10 = bf16[16,32,2560]{2,1,0:T(8,128)(2,1)S(1)} all-to-all(bf16[16,32,2560]{2,1,0:T(8,128)(2,1)S(1)} %bitcast.42), channel_id=1, replica_groups=mesh['groups'=2,'wide'=16,'narrow'=1] {'wide'}, dimensions={0} | all-to-all | bytes 5242880 | tf_op jit(solution)/shard_map/all_to_all | solution.py:25
  72.8 1.5 fusion.4
  74.3 0.0 copy-done.3
  74.3 1.5 fusion.9
  75.9 3.9 %fusion = f32[16,32,2560]{2,1,0:T(8,128)} fusion(bf16[16,32,384]{2,1,0:T(8,128)(2,1)S(1)} %bitcast.46, bf16[1,384,2560]{2,1,0:T(8,128)(2,1)S(1)} %copy-done), kind=kOutput, calls=%fused_computation.4 | convolution fusion | flops 1006632960 | bytes 7602176 | tf_op jit(solution)/shard_map/dot_general | solution.py:31
  79.8 5.3 %all-to-all-start.1 = ((f32[16,32,2560]{2,1,0:T(8,128)}), f32[16,32,2560]{2,1,0:T(8,128)}, u32[]{:S(2)}, u32[]{:S(2)}) async-start(f32[16,32,2560]{2,1,0:T(8,128)} %fusion), calls=%async_computation.1 | async-start | bytes 10485760 | tf_op jit(solution)/shard_map/all_to_all | solution.py:33
  85.1 0.1 copy.12
  85.2 0.1 mul.34
  85.3 114.7 %all-to-all-done.1 = f32[16,32,2560]{2,1,0:T(8,128)} async-done(((f32[16,32,2560]{2,1,0:T(8,128)}), f32[16,32,2560]{2,1,0:T(8,128)}, u32[]{:S(2)}, u32[]{:S(2)}) %all-to-all-start.1) | async-done | bytes 5242912 | tf_op jit(solution)/shard_map/all_to_all | solution.py:33
  200.0 3.2 %bitcast_reduce_fusion = bf16[8,32,2560]{2,1,0:T(8,128)(2,1)S(1)} fusion(f32[16,32,2560]{2,1,0:T(8,128)} %all-to-all-done.1), kind=kLoop, calls=%fused_computation.3 | loop fusion | flops 655360 | bytes 6553600 | tf_op jit(solution)/shard_map/reduce_sum | solution.py:34
  203.2 3.6 %gather_fusion.1 = bf16[128,2560]{1,0:T(8,128)(2,1)} fusion(bf16[8,32,2560]{2,1,0:T(8,128)(2,1)S(1)} %bitcast_reduce_fusion, s32[128]{0:T(128)S(1)} %get-tuple-element.5), kind=kCustom, calls=%fused_computation.1 | custom fusion | bytes 1311744 | tf_op jit(solution)/shard_map/gather | solution.py:35
  206.8 1.2 convert_multiply_fusion
  208.0 1.8 reshape.101
  209.9 3.6 %reduce_sum.29 = bf16[64,2560]{1,0:T(8,128)(2,1)} reduce(f32[64,2,2560]{2,1,0:T(2,128)} %reshape.101, f32[]{:T(128)} %constant.41.clone.1), dimensions={1}, to_apply=%region_4.5 | reduce | flops 163840 | bytes 1638404 | tf_op jit(solution)/shard_map/reduce_sum | solution.py:40
  (11 shorter events, 0.0 us)
Async XLA Ops:
  0.0 75.9 %copy-start = (bf16[1,384,2560]{2,1,0:T(8,128)(2,1)S(1)}, bf16[1,384,2560]{2,1,0:T(8,128)(2,1)}, u32[]{:S(2)}) copy-start(bf16[1,384,2560]{2,1,0:T(8,128)(2,1)} %param.11) | copy-start | bytes 5898244
  7.8 65.0 %copy-start.2 = (bf16[1,384,2560]{2,1,0:T(8,128)(2,1)S(1)}, bf16[1,384,2560]{2,1,0:T(8,128)(2,1)}, u32[]{:S(2)}) copy-start(bf16[1,384,2560]{2,1,0:T(8,128)(2,1)} %param.9) | copy-start | bytes 5898244
  72.8 1.5 copy-start.3
  79.8 5.3 %copy-start.1 = (f32[64,2]{0,1:T(2,128)S(1)}, f32[64,2]{0,1:T(2,128)}, u32[]{:S(2)}) copy-start(f32[64,2]{0,1:T(2,128)} %param.8) | copy-start | bytes 1540
  79.8 120.2 %all-to-all-start.1 = ((f32[16,32,2560]{2,1,0:T(8,128)}), f32[16,32,2560]{2,1,0:T(8,128)}, u32[]{:S(2)}, u32[]{:S(2)}) async-start(f32[16,32,2560]{2,1,0:T(8,128)} %fusion), calls=%async_computation.1 | async-start | bytes 10485760 | tf_op jit(solution)/shard_map/all_to_all | solution.py:33
where the time goes:
time: 214 us; the launch traced here: 213 us
  waiting for transfers between devices  115 us (54%)
  blocking collectives  65 us (30%)
  local copies, waits for them, and re-layouts  12.9 us (6%)
  other arithmetic  8.49 us (4%)
  matrix products  6.96 us (3%)
  starting transfers between devices  5.29 us (2%)
    all_to_all x1, waiting for transfers between devices, per_device(): lax.all_to_all(quarter_blocks, 'wide', split_axis=0, concat_axis=0, tiled...  115 us
    all_to_all x1, blocking collectives, per_device(): lax.all_to_all(outgoing, 'wide', split_axis=0, concat_axis=0, tiled=True)  65 us
    all_to_all x1, starting transfers between devices, per_device(): lax.all_to_all(quarter_blocks, 'wide', split_axis=0, concat_axis=0, tiled...  5.29 us
  transfers between devices with their start and end apart: 1, of which 1 were waited for; matrix products, arithmetic and copies ran while one was open for 0% of the time, Pallas kernels for 0%

commit v1 on v0

--- a/solution.py
+++ b/solution.py
@@ -1,7 +1,14 @@
+import functools
+
 import jax
 import jax.numpy as jnp
 from jax import lax
+from jax.experimental import pallas as pl
+from jax.experimental.pallas import tpu as pltpu
 from jax.sharding import PartitionSpec as P
+
+F32 = jnp.float32
+BF16 = jnp.bfloat16
 
 
 def per_device(tokens, expert_ids, route_weights, gate_weight, up_weight, down_weight):
@@ -41,6 +48,157 @@
     return mixed.astype(jnp.bfloat16)
 
 
+def flip(number, mask, bits):
+    out = number
+    for b in range(bits):
+        if (mask >> b) & 1:
+            bit = lax.rem(lax.div(number, 1 << b), 2)
+            out = out + (1 - 2 * bit) * (1 << b)
+    return out
+
+
+def kernel(chips, slots, groups_of, tok, ids, rw, gw, uw, dw, out,
+           sendbuf, recvbuf, outbuf, retbuf, gbuf, ubuf, dbuf, hid,
+           local_sem, w_send, w_recv, d_send, d_recv, r_send, r_recv):
+    bits = chips.bit_length() - 1
+    half = gw.shape[1]
+    width = tok.shape[1]
+    toks = tok.shape[0]
+    cols = chips * slots
+    tile = 512
+    me = lax.axis_index("wide")
+    chip = lax.div(me, 2)
+    core = lax.rem(me, 2)
+    sibling = 2 * chip + 1 - core
+    partner = [flip(chip, r, bits) for r in range(chips)]
+    device = [2 * p + core for p in partner]
+
+    barrier = pltpu.get_barrier_semaphore()
+    pl.semaphore_signal(barrier, inc=1, device_id={"wide": sibling}, device_id_type=pl.DeviceIdType.MESH)
+    for r in range(1, chips):
+        pl.semaphore_signal(barrier, inc=1, device_id={"wide": device[r]}, device_id_type=pl.DeviceIdType.MESH)
+
+    pairs = ((gw, gbuf), (uw, ubuf), (dw, dbuf))
+    local = [pltpu.make_async_copy(src.at[0], dst.at[pl.ds(0, half)], local_sem.at[i])
+             for i, (src, dst) in enumerate(pairs)]
+    for c in local:
+        c.start()
+
+    col = lax.broadcasted_iota(jnp.int32, (toks, cols), 1)
+    expert = jnp.zeros((toks, cols), jnp.int32)
+    first = jnp.zeros((toks, cols), jnp.int32)
+    for r in range(chips):
+        inside = (col >= r * slots) & (col < (r + 1) * slots)
+        expert = jnp.where(inside, partner[r], expert)
+        first = jnp.where(inside, r * slots, first)
+    pick0 = jnp.where(ids[:, 0:1] == expert, 1.0, 0.0)
+    pick1 = jnp.where(ids[:, 1:2] == expert, 1.0, 0.0)
+    named = pick0 + pick1
+    before = jnp.where(lax.broadcasted_iota(jnp.int32, (toks, toks), 0)
+                       > lax.broadcasted_iota(jnp.int32, (toks, toks), 1), 1.0, 0.0)
+    rank = jnp.dot(before.astype(BF16), named.astype(BF16), preferred_element_type=F32)
+    here = jnp.where(rank == (col - first).astype(F32), 1.0, 0.0)
+    choose = jnp.transpose(here * named).astype(BF16)
+    pick0 = (here * pick0).astype(BF16)
+    pick1 = (here * pick1).astype(BF16)
+
+    for at in range(0, width, tile):
+        picked = jnp.dot(choose, tok[:, at:at + tile], preferred_element_type=F32).astype(BF16)
+        sendbuf[:, at:at + tile] = picked
+        recvbuf[0:slots, at:at + tile] = picked[0:slots]
+
+    pl.semaphore_wait(barrier, chips)
+
+    dispatch, back = [None], [None]
+    for r in range(1, chips):
+        span = pl.ds(r * slots, slots)
+        dispatch.append(pltpu.make_async_remote_copy(
+            src_ref=sendbuf.at[span], dst_ref=recvbuf.at[span], send_sem=d_send.at[r], recv_sem=d_recv.at[r],
+            device_id={"wide": device[r]}, device_id_type=pl.DeviceIdType.MESH))
+        back.append(pltpu.make_async_remote_copy(
+            src_ref=outbuf.at[span], dst_ref=retbuf.at[span], send_sem=r_send.at[r], recv_sem=r_recv.at[r],
+            device_id={"wide": device[r]}, device_id_type=pl.DeviceIdType.MESH))
+    for r in range(chips - 1, 0, -1):
+        dispatch[r].start()
+    remote = [pltpu.make_async_remote_copy(
+        src_ref=src.at[0], dst_ref=dst.at[pl.ds(half, half)], send_sem=w_send.at[i], recv_sem=w_recv.at[i],
+        device_id={"wide": sibling}, device_id_type=pl.DeviceIdType.MESH) for i, (src, dst) in enumerate(pairs)]
+    for c in remote:
+        c.start()
+    for c in local:
+        c.wait()
+    for c in remote:
+        c.wait_recv()
+
+    hid_tile = 256
+    for low, high in groups_of:
+        for r in range(max(low, 1), high):
+            dispatch[r].wait_recv()
+        base, rows = low * slots, (high - low) * slots
+
+        @pl.loop(0, 2 * half // hid_tile)
+        def _(i):
+            at = pl.ds(pl.multiple_of(i * hid_tile, hid_tile), hid_tile)
+            x = recvbuf[base:base + rows, :]
+            dims = (((1,), (1,)), ((), ()))
+            gate = lax.dot_general(x, gbuf[at, :], dims, preferred_element_type=F32)
+            up = lax.dot_general(x, ubuf[at, :], dims, preferred_element_type=F32)
+            hid[base:base + rows, at] = (gate / (1.0 + jnp.exp(-gate)) * up).astype(BF16)
+
+        @pl.loop(0, width // tile)
+        def _(i):
+            at = pl.ds(pl.multiple_of(i * tile, tile), tile)
+            part = jnp.dot(hid[base:base + rows, :], dbuf[:, at], preferred_element_type=F32)
+            outbuf[base:base + rows, at] = part.astype(BF16)
+
+        for r in range(max(low, 1), high):
+            back[r].start()
+
+    retbuf[0:slots, :] = outbuf[0:slots, :]
+    for r in range(1, chips):
+        back[r].wait_recv()
+    for at in range(0, width, tile):
+        part = retbuf[:, at:at + tile]
+        total = (rw[:, 0:1] * jnp.dot(pick0, part, preferred_element_type=F32)
+                 + rw[:, 1:2] * jnp.dot(pick1, part, preferred_element_type=F32))
+        out[:, at:at + tile] = total.astype(BF16)
+
+    for c in remote:
+        c.wait_send()
+    for r in range(1, chips):
+        dispatch[r].wait_send()
+        back[r].wait_send()
+
+
+def fused(tokens, expert_ids, route_weights, gate_weight, up_weight, down_weight):
+    toks, width = tokens.shape
+    wide = lax.axis_size("wide")
+    chips = wide // 2
+    slots = 4 * toks * expert_ids.shape[1] // wide
+    half = gate_weight.shape[1]
+    rows = chips * slots
+    near = chips // 2
+    groups_of = ((0, near), (near, near + near // 2), (near + near // 2, chips))
+    vmem = pl.BlockSpec(memory_space=pltpu.VMEM)
+    hbm = pl.BlockSpec(memory_space=pl.ANY)
+    return pl.pallas_call(
+        functools.partial(kernel, chips, slots, groups_of),
+        out_shape=jax.ShapeDtypeStruct((toks, width), BF16),
+        in_specs=[vmem, vmem, vmem, hbm, hbm, hbm],
+        out_specs=vmem,
+        scratch_shapes=[pltpu.VMEM((rows, width), BF16)] * 4
+        + [pltpu.VMEM((2 * half, width), BF16)] * 3
+        + [pltpu.VMEM((rows, 2 * half), BF16)]
+        + [pltpu.SemaphoreType.DMA((3,))] * 3
+        + [pltpu.SemaphoreType.DMA((chips,))] * 4,
+        compiler_params=pltpu.CompilerParams(
+            collective_id=0, has_side_effects=True, vmem_limit_bytes=48 * 1024 * 1024),
+        cost_estimate=pl.CostEstimate(
+            flops=12 * rows * half * width, bytes_accessed=6 * half * width + 4 * toks * width,
+            transcendentals=2 * rows * half),
+    )(tokens, expert_ids, route_weights, gate_weight, up_weight, down_weight)
+
+
 def solution(mesh):
     in_specs = (
         P(("groups", "wide"), "narrow"),
@@ -51,6 +209,8 @@
         P("wide", "narrow", None),
     )
     out_specs = P(("groups", "wide"), "narrow")
+    chips = mesh.shape["wide"] // 2
+    whole_rows = mesh.shape["narrow"] == 1 and chips >= 4 and chips & (chips - 1) == 0
     return jax.shard_map(
-        per_device, mesh=mesh, in_specs=in_specs, out_specs=out_specs, check_vma=False
+        fused if whole_rows else per_device, mesh=mesh, in_specs=in_specs, out_specs=out_specs, check_vma=False
     )

time: 214 us -> 72 us (0.34)
  the two profiles are of different devices: /device:TPU:11 before, /device:TPU:8 now
where the time goes in v1:
time: 72 us; the launch traced here: 71.8 us
  Pallas kernels  65.4 us (91%)
  local copies, waits for them, and re-layouts  6.32 us (9%)
    pallas_call x1, Pallas kernels, fused(): pl.pallas_call(functools.partial(kernel, chips, slots, groups_of), out_sh...  65.4 us
    unnamed x9, local copies, waits for them, and re-layouts  6.32 us

profile of v1, /device:TPU:8, one launch (start us, length us, event | category | flops | bytes accessed | tf_op | source)
XLA Modules:
  0.0 71.8 jit_solution(4155028360240027066)
XLA Ops:
  0.0 0.8 %copy.7.ids = s32[64,2]{1,0:T(8,128)S(1)} copy(s32[64,2]{0,1:T(2,128)} %param.7) | data formatting | bytes 1024 | tf_op args[1]
  0.8 0.8 %copy.8.rw = f32[64,2]{1,0:T(8,128)S(1)} copy(f32[64,2]{0,1:T(2,128)} %param.8) | data formatting | bytes 1024 | tf_op args[2]
  1.5 0.0 copy-start
  1.5 1.5 %copy-done = bf16[1,384,2560]{2,1,0:T(8,128)(2,1)S(1)} copy-done((bf16[1,384,2560]{2,1,0:T(8,128)(2,1)S(1)}, bf16[1,384,2560]{2,1,0:T(8,128)(2,1)}, u32[]{:S(2)}) %copy-start) | copy-done | bytes 1966104
  3.1 0.0 copy-start.1
  3.1 1.5 %copy-done.1 = bf16[1,384,2560]{2,1,0:T(8,128)(2,1)S(1)} copy-done((bf16[1,384,2560]{2,1,0:T(8,128)(2,1)S(1)}, bf16[1,384,2560]{2,1,0:T(8,128)(2,1)}, u32[]{:S(2)}) %copy-start.1) | copy-done | bytes 1966104
  4.6 0.0 copy-start.2
  4.6 1.0 %copy-done.2 = bf16[64,2560]{1,0:T(8,128)(2,1)S(1)} copy-done((bf16[64,2560]{1,0:T(8,128)(2,1)S(1)}, bf16[64,2560]{1,0:T(8,128)(2,1)}, u32[]{:S(2)}) %copy-start.2) | copy-done | bytes 327704
  5.6 65.4 %shard_map.64 = bf16[64,2560]{1,0:T(8,128)(2,1)S(1)} custom-call(bf16[64,2560]{1,0:T(8,128)(2,1)S(1)} %copy-done.2, s32[64,2]{1,0:T(8,128)S(1)} %copy.7.ids, f32[64,2]{1,0:T(8,128)S(1)} %copy.8.rw, bf16[1,384,2560]{2,1,0:T(8,128)(2,1)S(1)} %copy-done, bf16[1,384,2560]{2,1,0:T(8,128)(2,1)S(1)} %copy-done.1, bf16[1,384,2560]{2,1,0:T(8,128)(2,1)} %dw.1), custom_call_target="tpu_custom_call" | custom-call | flops 3019898880 | bytes 6553600 | tf_op jit(solution)/shard_map/pallas_call | solution.py:184
  71.0 0.7 %copy.10 = bf16[64,2560]{1,0:T(8,128)(2,1)} copy(bf16[64,2560]{1,0:T(8,128)(2,1)S(1)} %shard_map.64) | data formatting | bytes 655360
Async XLA Ops:
  1.5 1.5 %copy-start = (bf16[1,384,2560]{2,1,0:T(8,128)(2,1)S(1)}, bf16[1,384,2560]{2,1,0:T(8,128)(2,1)}, u32[]{:S(2)}) copy-start(bf16[1,384,2560]{2,1,0:T(8,128)(2,1)} %gw.1) | copy-start | bytes 5898244
  3.1 1.5 %copy-start.1 = (bf16[1,384,2560]{2,1,0:T(8,128)(2,1)S(1)}, bf16[1,384,2560]{2,1,0:T(8,128)(2,1)}, u32[]{:S(2)}) copy-start(bf16[1,384,2560]{2,1,0:T(8,128)(2,1)} %uw.1) | copy-start | bytes 5898244
  4.6 1.0 %copy-start.2 = (bf16[64,2560]{1,0:T(8,128)(2,1)S(1)}, bf16[64,2560]{1,0:T(8,128)(2,1)}, u32[]{:S(2)}) copy-start(bf16[64,2560]{1,0:T(8,128)(2,1)} %tok.1) | copy-start | bytes 983044

commit v2 on v0

--- a/solution.py
+++ b/solution.py
@@ -1,7 +1,14 @@
+import functools
+
 import jax
 import jax.numpy as jnp
 from jax import lax
+from jax.experimental import pallas as pl
+from jax.experimental.pallas import tpu as pltpu
 from jax.sharding import PartitionSpec as P
+
+F32 = jnp.float32
+BF16 = jnp.bfloat16
 
 
 def per_device(tokens, expert_ids, route_weights, gate_weight, up_weight, down_weight):
@@ -41,6 +48,236 @@
     return mixed.astype(jnp.bfloat16)
 
 
+def flip(number, mask, bits):
+    out = number
+    for b in range(bits):
+        if (mask >> b) & 1:
+            bit = lax.rem(lax.div(number, 1 << b), 2)
+            out = out + (1 - 2 * bit) * (1 << b)
+    return out
+
+
+def column(row):
+    n = row.shape[1]
+    same = lax.broadcasted_iota(jnp.int32, (n, n), 0) == lax.broadcasted_iota(jnp.int32, (n, n), 1)
+    return jnp.sum(jnp.where(same, row, 0.0), axis=1, keepdims=True)
+
+
+def one_hots(ids, experts, slots):
+    toks = ids.shape[1]
+    cols = len(experts) * slots
+    id0 = column(ids[0:1, :].astype(F32))
+    id1 = column(ids[1:2, :].astype(F32))
+    col = lax.broadcasted_iota(jnp.int32, (toks, cols), 1)
+    expert = jnp.zeros((toks, cols), F32)
+    first = jnp.zeros((toks, cols), jnp.int32)
+    for r, e in enumerate(experts):
+        inside = (col >= r * slots) & (col < (r + 1) * slots)
+        expert = jnp.where(inside, e.astype(F32), expert)
+        first = jnp.where(inside, r * slots, first)
+    pick0 = jnp.where(id0 == expert, 1.0, 0.0)
+    pick1 = jnp.where(id1 == expert, 1.0, 0.0)
+    named = pick0 + pick1
+    before = jnp.where(lax.broadcasted_iota(jnp.int32, (toks, toks), 0)
+                       > lax.broadcasted_iota(jnp.int32, (toks, toks), 1), 1.0, 0.0)
+    rank = jnp.dot(before.astype(BF16), named.astype(BF16), preferred_element_type=F32)
+    here = jnp.where(rank == (col - first).astype(F32), 1.0, 0.0)
+    choose = jnp.transpose(here * named).astype(BF16)
+    return choose, (here * pick0).astype(BF16), (here * pick1).astype(BF16)
+
+
+def kernel(chips, slots, tile, tok, ids, rw, gw, uw, dw, out,
+           tokbuf, idbuf, rwbuf, fartok, farid, farrw, nearsend, relaysend, recvbuf, outbuf,
+           nearret, farret, mixfar, mixback, nearsum, gbuf, ubuf, dbuf, hid,
+           local_sem, w_send, w_recv, t_send, t_recv, m_send, m_recv, n_send, n_recv,
+           l_send, l_recv, b_send, b_recv, f_send, f_recv, c_send, c_recv):
+    bits = chips.bit_length() - 1
+    near = chips // 2
+    half = gw.shape[1]
+    width = tok.shape[1]
+    chunks = width // tile
+    mine = near * slots
+    me = lax.axis_index("wide")
+    chip = lax.div(me, 2)
+    core = lax.rem(me, 2)
+    sibling = 2 * chip + 1 - core
+    partner = [flip(chip, r, bits) for r in range(near)]
+    device = [2 * p + core for p in partner]
+    across = 2 * flip(chip, near, bits) + core
+
+    def remote(src, dst, send, recv, to):
+        return pltpu.make_async_remote_copy(src_ref=src, dst_ref=dst, send_sem=send, recv_sem=recv,
+                                            device_id={"wide": to}, device_id_type=pl.DeviceIdType.MESH)
+
+    barrier = pltpu.get_barrier_semaphore()
+    for to in [across, sibling] + device[1:]:
+        pl.semaphore_signal(barrier, inc=1, device_id={"wide": to}, device_id_type=pl.DeviceIdType.MESH)
+
+    pairs = ((gw, gbuf), (uw, ubuf), (dw, dbuf))
+    small = [pltpu.make_async_copy(src, dst, local_sem.at[3 + i])
+             for i, (src, dst) in enumerate(((ids, idbuf), (rw, rwbuf), (tok, tokbuf)))]
+    local = [pltpu.make_async_copy(src.at[0], dst.at[pl.ds(0, half)], local_sem.at[i])
+             for i, (src, dst) in enumerate(pairs)]
+    for c in small + local:
+        c.start()
+    for c in small:
+        c.wait()
+
+    choose, near0, near1 = one_hots(idbuf, partner, slots)
+    for c in range(chunks):
+        cut = slice(c * tile, (c + 1) * tile)
+        picked = jnp.dot(choose, tokbuf[:, cut], preferred_element_type=F32).astype(BF16)
+        nearsend[:, cut] = picked
+        recvbuf[0:slots, cut] = picked[0:slots]
+
+    pl.semaphore_wait(barrier, near + 1)
+
+    span = [pl.ds(r * slots, slots) for r in range(chips)]
+    cuts = [pl.ds(c * tile, tile) for c in range(chunks)]
+    meta = [remote(idbuf, farid, m_send.at[0], m_recv.at[0], across),
+            remote(rwbuf, farrw, m_send.at[1], m_recv.at[1], across)]
+    over = [remote(tokbuf.at[:, cuts[c]], fartok.at[:, cuts[c]], t_send.at[c], t_recv.at[c], across)
+            for c in range(chunks)]
+    swap = [remote(src.at[0], dst.at[pl.ds(half, half)], w_send.at[i], w_recv.at[i], sibling)
+            for i, (src, dst) in enumerate(pairs)]
+    direct = [remote(nearsend.at[span[r]], recvbuf.at[span[r]], n_send.at[r], n_recv.at[r], device[r])
+              for r in range(1, near)]
+    relay = [[remote(relaysend.at[span[r], cuts[c]], recvbuf.at[span[near + r], cuts[c]],
+                     l_send.at[r, c], l_recv.at[r, c], device[r]) for r in range(1, near)] for c in range(chunks)]
+    back = [remote(outbuf.at[span[r]], nearret.at[span[r]], b_send.at[r], b_recv.at[r], device[r])
+            for r in range(1, near)]
+    farback = [[remote(outbuf.at[span[near + r], cuts[c]], farret.at[span[r], cuts[c]],
+                       f_send.at[r, c], f_recv.at[r, c], device[r]) for r in range(1, near)] for c in range(chunks)]
+    home = [remote(mixfar.at[:, cuts[c]], mixback.at[:, cuts[c]], c_send.at[c], c_recv.at[c], across)
+            for c in range(chunks)]
+
+    for c in meta + over + swap + direct:
+        c.start()
+
+    for c in meta:
+        c.wait_recv()
+    choose, far0, far1 = one_hots(farid, partner, slots)
+    for c in range(chunks):
+        cut = slice(c * tile, (c + 1) * tile)
+        over[c].wait_recv()
+        picked = jnp.dot(choose, fartok[:, cut], preferred_element_type=F32).astype(BF16)
+        relaysend[:, cut] = picked
+        recvbuf[mine:mine + slots, cut] = picked[0:slots]
+        for copy in relay[c]:
+            copy.start()
+
+    for c in local:
+        c.wait()
+    for c in swap:
+        c.wait_recv()
+
+    hid_tile = 256
+
+    def into_hidden(base):
+        @pl.loop(0, 2 * half // hid_tile)
+        def _(i):
+            at = pl.ds(pl.multiple_of(i * hid_tile, hid_tile), hid_tile)
+            x = recvbuf[base:base + mine, :]
+            dims = (((1,), (1,)), ((), ()))
+            gate = lax.dot_general(x, gbuf[at, :], dims, preferred_element_type=F32)
+            up = lax.dot_general(x, ubuf[at, :], dims, preferred_element_type=F32)
+            hid[:, at] = (gate / (1.0 + jnp.exp(-gate)) * up).astype(BF16)
+
+    for c in direct:
+        c.wait_recv()
+    into_hidden(0)
+    for c in range(chunks):
+        cut = slice(c * tile, (c + 1) * tile)
+        part = jnp.dot(hid[...], dbuf[:, cut], preferred_element_type=F32).astype(BF16)
+        outbuf[0:mine, cut] = part
+        nearret[0:slots, cut] = part[0:slots]
+    for c in back:
+        c.start()
+
+    for c in range(chunks):
+        for copy in relay[c]:
+            copy.wait_recv()
+    into_hidden(mine)
+    for c in range(chunks):
+        cut = slice(c * tile, (c + 1) * tile)
+        part = jnp.dot(hid[...], dbuf[:, cut], preferred_element_type=F32).astype(BF16)
+        outbuf[mine:2 * mine, cut] = part
+        farret[0:slots, cut] = part[0:slots]
+        for copy in farback[c]:
+            copy.start()
+
+    w0, w1 = column(farrw[0:1, :]), column(farrw[1:2, :])
+    for c in range(chunks):
+        cut = slice(c * tile, (c + 1) * tile)
+        for copy in farback[c]:
+            copy.wait_recv()
+        part = farret[:, cut]
+        mixfar[:, cut] = (w0 * jnp.dot(far0, part, preferred_element_type=F32)
+                          + w1 * jnp.dot(far1, part, preferred_element_type=F32)).astype(BF16)
+        home[c].start()
+
+    w0, w1 = column(rwbuf[0:1, :]), column(rwbuf[1:2, :])
+    for c in back:
+        c.wait_recv()
+    for c in range(chunks):
+        cut = slice(c * tile, (c + 1) * tile)
+        part = nearret[:, cut]
+        nearsum[:, cut] = (w0 * jnp.dot(near0, part, preferred_element_type=F32)
+                           + w1 * jnp.dot(near1, part, preferred_element_type=F32))
+    for c in range(chunks):
+        cut = slice(c * tile, (c + 1) * tile)
+        home[c].wait_recv()
+        out[:, cut] = (nearsum[:, cut] + mixback[:, cut].astype(F32)).astype(BF16)
+
+    for c in meta + over + swap + direct + back + home:
+        c.wait_send()
+    for c in range(chunks):
+        for copy in relay[c] + farback[c]:
+            copy.wait_send()
+
+
+def fused(tokens, expert_ids, route_weights, gate_weight, up_weight, down_weight):
+    toks, width = tokens.shape
+    picks = expert_ids.shape[1]
+    wide = lax.axis_size("wide")
+    chips = wide // 2
+    near = chips // 2
+    slots = 4 * toks * picks // wide
+    half = gate_weight.shape[1]
+    rows = chips * slots
+    mine = near * slots
+    tile = 512
+    chunks = width // tile
+    vmem = pl.BlockSpec(memory_space=pltpu.VMEM)
+    hbm = pl.BlockSpec(memory_space=pl.ANY)
+    tok_like = pltpu.VMEM((toks, width), BF16)
+    near_like = pltpu.VMEM((mine, width), BF16)
+    all_like = pltpu.VMEM((rows, width), BF16)
+    id_like = pltpu.VMEM((picks, toks), jnp.int32)
+    rw_like = pltpu.VMEM((picks, toks), F32)
+    sems = pltpu.SemaphoreType.DMA
+    return pl.pallas_call(
+        functools.partial(kernel, chips, slots, tile),
+        out_shape=jax.ShapeDtypeStruct((toks, width), BF16),
+        in_specs=[hbm] * 6,
+        out_specs=vmem,
+        scratch_shapes=[tok_like, id_like, rw_like, tok_like, id_like, rw_like, near_like, near_like,
+                        all_like, all_like, near_like, near_like, tok_like, tok_like,
+                        pltpu.VMEM((toks, width), F32)]
+        + [pltpu.VMEM((2 * half, width), BF16)] * 3
+        + [pltpu.VMEM((mine, 2 * half), BF16)]
+        + [sems((6,)), sems((3,)), sems((3,)), sems((chunks,)), sems((chunks,)), sems((2,)), sems((2,)),
+           sems((near,)), sems((near,)), sems((near, chunks)), sems((near, chunks)),
+           sems((near,)), sems((near,)), sems((near, chunks)), sems((near, chunks)),
+           sems((chunks,)), sems((chunks,))],
+        compiler_params=pltpu.CompilerParams(
+            collective_id=0, has_side_effects=True, vmem_limit_bytes=60 * 1024 * 1024),
+        cost_estimate=pl.CostEstimate(
+            flops=12 * rows * half * width, bytes_accessed=6 * half * width + 4 * toks * width,
+            transcendentals=2 * rows * half),
+    )(tokens, expert_ids.T, route_weights.T, gate_weight, up_weight, down_weight)
+
+
 def solution(mesh):
     in_specs = (
         P(("groups", "wide"), "narrow"),
@@ -51,6 +288,8 @@
         P("wide", "narrow", None),
     )
     out_specs = P(("groups", "wide"), "narrow")
+    chips = mesh.shape["wide"] // 2
+    whole_rows = mesh.shape["narrow"] == 1 and chips >= 4 and chips & (chips - 1) == 0
     return jax.shard_map(
-        per_device, mesh=mesh, in_specs=in_specs, out_specs=out_specs, check_vma=False
+        fused if whole_rows else per_device, mesh=mesh, in_specs=in_specs, out_specs=out_specs, check_vma=False
     )

time: 214 us -> 57.5 us (0.27)
  the two profiles are of different devices: /device:TPU:11 before, /device:TPU:0 now
where the time goes in v2:
time: 57.5 us; the launch traced here: 57.3 us
  Pallas kernels  55.6 us (97%)
  local copies, waits for them, and re-layouts  1.72 us (3%)
    pallas_call x1, Pallas kernels, fused(): pl.pallas_call(functools.partial(kernel, chips, slots, tile), out_shape=j...  55.6 us
    unnamed x1, local copies, waits for them, and re-layouts  1.72 us

profile of v2, /device:TPU:0, one launch (start us, length us, event | category | flops | bytes accessed | tf_op | source)
XLA Modules:
  0.0 57.3 jit_solution(11380832490715541848)
XLA Ops:
  0.0 55.6 %shard_map.64 = bf16[64,2560]{1,0:T(8,128)(2,1)} custom-call(bf16[64,2560]{1,0:T(8,128)(2,1)} %tok.1, s32[2,64]{1,0:T(2,128)} %bitcast.2, f32[2,64]{1,0:T(2,128)} %bitcast.3, bf16[1,384,2560]{2,1,0:T(8,128)(2,1)} %gw.1, bf16[1,384,2560]{2,1,0:T(8,128)(2,1)} %uw.1, bf16[1,384,2560]{2,1,0:T(8,128)(2,1)} %dw.1), custom_call_target="tpu_custom_call" | custom-call | flops 3019898880 | bytes 6553600 | tf_op jit(solution)/shard_map/pallas_call | solution.py:259
  55.6 1.7 %copy.8 = bf16[64,2560]{1,0:T(8,128)(2,1)} copy(bf16[64,2560]{1,0:T(8,128)(2,1)} %shard_map.64) | data formatting | bytes 655360

commit v3 on v2

--- a/solution.py
+++ b/solution.py
@@ -120,23 +120,12 @@
              for i, (src, dst) in enumerate(pairs)]
     for c in small + local:
         c.start()
-    for c in small:
-        c.wait()
-
-    choose, near0, near1 = one_hots(idbuf, partner, slots)
-    for c in range(chunks):
-        cut = slice(c * tile, (c + 1) * tile)
-        picked = jnp.dot(choose, tokbuf[:, cut], preferred_element_type=F32).astype(BF16)
-        nearsend[:, cut] = picked
-        recvbuf[0:slots, cut] = picked[0:slots]
-
-    pl.semaphore_wait(barrier, near + 1)
 
     span = [pl.ds(r * slots, slots) for r in range(chips)]
     cuts = [pl.ds(c * tile, tile) for c in range(chunks)]
-    meta = [remote(idbuf, farid, m_send.at[0], m_recv.at[0], across),
-            remote(rwbuf, farrw, m_send.at[1], m_recv.at[1], across)]
-    over = [remote(tokbuf.at[:, cuts[c]], fartok.at[:, cuts[c]], t_send.at[c], t_recv.at[c], across)
+    meta = [remote(ids, farid, m_send.at[0], m_recv.at[0], across),
+            remote(rw, farrw, m_send.at[1], m_recv.at[1], across)]
+    over = [remote(tok.at[:, cuts[c]], fartok.at[:, cuts[c]], t_send.at[c], t_recv.at[c], across)
             for c in range(chunks)]
     swap = [remote(src.at[0], dst.at[pl.ds(half, half)], w_send.at[i], w_recv.at[i], sibling)
             for i, (src, dst) in enumerate(pairs)]
@@ -151,7 +140,19 @@
     home = [remote(mixfar.at[:, cuts[c]], mixback.at[:, cuts[c]], c_send.at[c], c_recv.at[c], across)
             for c in range(chunks)]
 
-    for c in meta + over + swap + direct:
+    pl.semaphore_wait(barrier, near + 1)
+    for c in meta + over:
+        c.start()
+
+    for c in small:
+        c.wait()
+    choose, near0, near1 = one_hots(idbuf, partner, slots)
+    for c in range(chunks):
+        cut = slice(c * tile, (c + 1) * tile)
+        picked = jnp.dot(choose, tokbuf[:, cut], preferred_element_type=F32).astype(BF16)
+        nearsend[:, cut] = picked
+        recvbuf[0:slots, cut] = picked[0:slots]
+    for c in direct + swap:
         c.start()
 
     for c in meta:

time: 57.5 us -> 56.8 us (0.988)
  Pallas kernels: 55.6 us -> 55 us
    pallas_call x1, Pallas kernels: 55.6 us -> 55 us  [fused(): pl.pallas_call(functools.partial(kernel, chips, slots, tile), out_shape=j...]
where the time goes in v3:
time: 56.8 us; the launch traced here: 56.7 us
  Pallas kernels  55 us (97%)
  local copies, waits for them, and re-layouts  1.72 us (3%)
    pallas_call x1, Pallas kernels, fused(): pl.pallas_call(functools.partial(kernel, chips, slots, tile), out_shape=j...  55 us
    unnamed x1, local copies, waits for them, and re-layouts  1.72 us

profile of v3, /device:TPU:0, one launch (start us, length us, event | category | flops | bytes accessed | tf_op | source)
XLA Modules:
  0.0 56.7 jit_solution(6961980503249593593)
XLA Ops:
  0.0 55.0 %shard_map.64 = bf16[64,2560]{1,0:T(8,128)(2,1)} custom-call(bf16[64,2560]{1,0:T(8,128)(2,1)} %tok.1, s32[2,64]{1,0:T(2,128)} %bitcast.2, f32[2,64]{1,0:T(2,128)} %bitcast.3, bf16[1,384,2560]{2,1,0:T(8,128)(2,1)} %gw.1, bf16[1,384,2560]{2,1,0:T(8,128)(2,1)} %uw.1, bf16[1,384,2560]{2,1,0:T(8,128)(2,1)} %dw.1), custom_call_target="tpu_custom_call" | custom-call | flops 3019898880 | bytes 6553600 | tf_op jit(solution)/shard_map/pallas_call | solution.py:260
  55.0 1.7 %copy.8 = bf16[64,2560]{1,0:T(8,128)(2,1)} copy(bf16[64,2560]{1,0:T(8,128)(2,1)} %shard_map.64) | data formatting | bytes 655360

commit v4 on v3

--- a/solution.py
+++ b/solution.py
@@ -247,7 +247,7 @@
     half = gate_weight.shape[1]
     rows = chips * slots
     mine = near * slots
-    tile = 512
+    tile = 256
     chunks = width // tile
     vmem = pl.BlockSpec(memory_space=pltpu.VMEM)
     hbm = pl.BlockSpec(memory_space=pl.ANY)

time: 56.8 us -> 57.1 us (level)
  no operation moved by 1% of the time
where the time goes in v4:
time: 57.1 us; the launch traced here: 56.9 us
  Pallas kernels  55.2 us (97%)
  local copies, waits for them, and re-layouts  1.72 us (3%)
    pallas_call x1, Pallas kernels, fused(): pl.pallas_call(functools.partial(kernel, chips, slots, tile), out_shape=j...  55.2 us
    unnamed x1, local copies, waits for them, and re-layouts  1.72 us

profile of v4, /device:TPU:0, one launch (start us, length us, event | category | flops | bytes accessed | tf_op | source)
XLA Modules:
  0.0 56.9 jit_solution(5711547274664255232)
XLA Ops:
  0.0 55.2 %shard_map.64 = bf16[64,2560]{1,0:T(8,128)(2,1)} custom-call(bf16[64,2560]{1,0:T(8,128)(2,1)} %tok.1, s32[2,64]{1,0:T(2,128)} %bitcast.2, f32[2,64]{1,0:T(2,128)} %bitcast.3, bf16[1,384,2560]{2,1,0:T(8,128)(2,1)} %gw.1, bf16[1,384,2560]{2,1,0:T(8,128)(2,1)} %uw.1, bf16[1,384,2560]{2,1,0:T(8,128)(2,1)} %dw.1), custom_call_target="tpu_custom_call" | custom-call | flops 3019898880 | bytes 6553600 | tf_op jit(solution)/shard_map/pallas_call | solution.py:260
  55.2 1.7 %copy.8 = bf16[64,2560]{1,0:T(8,128)(2,1)} copy(bf16[64,2560]{1,0:T(8,128)(2,1)} %shard_map.64) | data formatting | bytes 655360

commit v5 on v3

--- a/solution.py
+++ b/solution.py
@@ -86,13 +86,12 @@
     return choose, (here * pick0).astype(BF16), (here * pick1).astype(BF16)
 
 
-def kernel(chips, slots, tile, tok, ids, rw, gw, uw, dw, out,
+def kernel(slots, tile, tok, ids, rw, gw, uw, dw, out,
            tokbuf, idbuf, rwbuf, fartok, farid, farrw, nearsend, relaysend, recvbuf, outbuf,
            nearret, farret, mixfar, mixback, nearsum, gbuf, ubuf, dbuf, hid,
            local_sem, w_send, w_recv, t_send, t_recv, m_send, m_recv, n_send, n_recv,
            l_send, l_recv, b_send, b_recv, f_send, f_recv, c_send, c_recv):
-    bits = chips.bit_length() - 1
-    near = chips // 2
+    near = 4
     half = gw.shape[1]
     width = tok.shape[1]
     chunks = width // tile
@@ -100,17 +99,22 @@
     me = lax.axis_index("wide")
     chip = lax.div(me, 2)
     core = lax.rem(me, 2)
+    z = lax.div(chip, 2)
+    inner = lax.rem(z + 1, 4) >= 2
+    outer = lax.rem(z + 1, 4) < 2
+    slot = jnp.where(inner, 0, 1)
     sibling = 2 * chip + 1 - core
-    partner = [flip(chip, r, bits) for r in range(near)]
+    partner = [flip(chip, r, 3) for r in range(near)]
     device = [2 * p + core for p in partner]
-    across = 2 * flip(chip, near, bits) + core
+    across = [2 * flip(chip, 6, 3) + core, 2 * flip(chip, 4, 3) + core]
+    relay_of_me = jnp.where(inner, across[0], across[1])
 
     def remote(src, dst, send, recv, to):
         return pltpu.make_async_remote_copy(src_ref=src, dst_ref=dst, send_sem=send, recv_sem=recv,
                                             device_id={"wide": to}, device_id_type=pl.DeviceIdType.MESH)
 
     barrier = pltpu.get_barrier_semaphore()
-    for to in [across, sibling] + device[1:]:
+    for to in across + [sibling] + device[1:]:
         pl.semaphore_signal(barrier, inc=1, device_id={"wide": to}, device_id_type=pl.DeviceIdType.MESH)
 
     pairs = ((gw, gbuf), (uw, ubuf), (dw, dbuf))
@@ -121,28 +125,43 @@
     for c in small + local:
         c.start()
 
-    span = [pl.ds(r * slots, slots) for r in range(chips)]
+    span = [pl.ds(r * slots, slots) for r in range(2 * near)]
     cuts = [pl.ds(c * tile, tile) for c in range(chunks)]
-    meta = [remote(ids, farid, m_send.at[0], m_recv.at[0], across),
-            remote(rw, farrw, m_send.at[1], m_recv.at[1], across)]
-    over = [remote(tok.at[:, cuts[c]], fartok.at[:, cuts[c]], t_send.at[c], t_recv.at[c], across)
-            for c in range(chunks)]
+    sides = range(2)
+
+    def crossing(at):
+        meta = [remote(ids, farid.at[at], m_send.at[0], m_recv.at[at, 0], relay_of_me),
+                remote(rw, farrw.at[at], m_send.at[1], m_recv.at[at, 1], relay_of_me)]
+        return meta, [remote(tok.at[:, cuts[c]], fartok.at[at, :, cuts[c]], t_send.at[c], t_recv.at[at, c],
+                             relay_of_me) for c in range(chunks)]
+
+    meta, over = crossing(slot)
+    arriving = [crossing(g) for g in sides]
     swap = [remote(src.at[0], dst.at[pl.ds(half, half)], w_send.at[i], w_recv.at[i], sibling)
             for i, (src, dst) in enumerate(pairs)]
     direct = [remote(nearsend.at[span[r]], recvbuf.at[span[r]], n_send.at[r], n_recv.at[r], device[r])
               for r in range(1, near)]
-    relay = [[remote(relaysend.at[span[r], cuts[c]], recvbuf.at[span[near + r], cuts[c]],
-                     l_send.at[r, c], l_recv.at[r, c], device[r]) for r in range(1, near)] for c in range(chunks)]
     back = [remote(outbuf.at[span[r]], nearret.at[span[r]], b_send.at[r], b_recv.at[r], device[r])
             for r in range(1, near)]
-    farback = [[remote(outbuf.at[span[near + r], cuts[c]], farret.at[span[r], cuts[c]],
-                       f_send.at[r, c], f_recv.at[r, c], device[r]) for r in range(1, near)] for c in range(chunks)]
-    home = [remote(mixfar.at[:, cuts[c]], mixback.at[:, cuts[c]], c_send.at[c], c_recv.at[c], across)
-            for c in range(chunks)]
-
-    pl.semaphore_wait(barrier, near + 1)
-    for c in meta + over:
-        c.start()
+
+    def block(g, i):
+        return span[near + 2 * g + i]
+
+    relay = [[[remote(relaysend.at[g, span[r], cuts[c]], recvbuf.at[block(g, r % 2), cuts[c]],
+                      l_send.at[g, r, c], l_recv.at[g, r % 2, c], device[r]) for r in (2, 3, 1)]
+              for c in range(chunks)] for g in sides]
+    answer = [[[None] + [remote(outbuf.at[block(g, r % 2), cuts[c]], farret.at[g, span[r], cuts[c]],
+                                f_send.at[g, r % 2, c], f_recv.at[g, r, c], device[r]) for r in range(1, near)]
+               for c in range(chunks)] for g in sides]
+    home = [[remote(mixfar.at[g, :, cuts[c]], mixback.at[:, cuts[c]], c_send.at[g, c], c_recv.at[c], across[g])
+             for c in range(chunks)] for g in sides]
+
+    pl.semaphore_wait(barrier, near + 2)
+
+    @pl.when(inner)
+    def _():
+        for c in meta + over:
+            c.start()
 
     for c in small:
         c.wait()
@@ -152,20 +171,32 @@
         picked = jnp.dot(choose, tokbuf[:, cut], preferred_element_type=F32).astype(BF16)
         nearsend[:, cut] = picked
         recvbuf[0:slots, cut] = picked[0:slots]
-    for c in direct + swap:
+    for c in direct:
         c.start()
 
-    for c in meta:
-        c.wait_recv()
-    choose, far0, far1 = one_hots(farid, partner, slots)
-    for c in range(chunks):
-        cut = slice(c * tile, (c + 1) * tile)
-        over[c].wait_recv()
-        picked = jnp.dot(choose, fartok[:, cut], preferred_element_type=F32).astype(BF16)
-        relaysend[:, cut] = picked
-        recvbuf[mine:mine + slots, cut] = picked[0:slots]
-        for copy in relay[c]:
-            copy.start()
+    @pl.when(outer)
+    def _():
+        for c in meta + over:
+            c.start()
+
+    for c in swap:
+        c.start()
+
+    @pl.when(inner)
+    def _():
+        for g in sides:
+            for c in arriving[g][0]:
+                c.wait_recv()
+            choose, unused0, unused1 = one_hots(farid.at[g], partner, slots)
+            for c in range(chunks):
+                cut = slice(c * tile, (c + 1) * tile)
+                arriving[g][1][c].wait_recv()
+                picked = jnp.dot(choose, fartok[g, :, cut], preferred_element_type=F32).astype(BF16)
+                relaysend[g, :, cut] = picked
+                low = mine + 2 * g * slots
+                recvbuf[low:low + slots, cut] = picked[0:slots]
+                for copy in relay[g][c]:
+                    copy.start()
 
     for c in local:
         c.wait()
@@ -174,19 +205,19 @@
 
     hid_tile = 256
 
-    def into_hidden(base):
+    def into_hidden(base, rows):
         @pl.loop(0, 2 * half // hid_tile)
         def _(i):
             at = pl.ds(pl.multiple_of(i * hid_tile, hid_tile), hid_tile)
-            x = recvbuf[base:base + mine, :]
+            x = recvbuf[base:base + rows, :]
             dims = (((1,), (1,)), ((), ()))
             gate = lax.dot_general(x, gbuf[at, :], dims, preferred_element_type=F32)
             up = lax.dot_general(x, ubuf[at, :], dims, preferred_element_type=F32)
-            hid[:, at] = (gate / (1.0 + jnp.exp(-gate)) * up).astype(BF16)
+            hid[0:rows, at] = (gate / (1.0 + jnp.exp(-gate)) * up).astype(BF16)
 
     for c in direct:
         c.wait_recv()
-    into_hidden(0)
+    into_hidden(0, mine)
     for c in range(chunks):
         cut = slice(c * tile, (c + 1) * tile)
         part = jnp.dot(hid[...], dbuf[:, cut], preferred_element_type=F32).astype(BF16)
@@ -195,27 +226,45 @@
     for c in back:
         c.start()
 
-    for c in range(chunks):
-        for copy in relay[c]:
-            copy.wait_recv()
-    into_hidden(mine)
-    for c in range(chunks):
-        cut = slice(c * tile, (c + 1) * tile)
-        part = jnp.dot(hid[...], dbuf[:, cut], preferred_element_type=F32).astype(BF16)
-        outbuf[mine:2 * mine, cut] = part
-        farret[0:slots, cut] = part[0:slots]
-        for copy in farback[c]:
-            copy.start()
-
-    w0, w1 = column(farrw[0:1, :]), column(farrw[1:2, :])
-    for c in range(chunks):
-        cut = slice(c * tile, (c + 1) * tile)
-        for copy in farback[c]:
-            copy.wait_recv()
-        part = farret[:, cut]
-        mixfar[:, cut] = (w0 * jnp.dot(far0, part, preferred_element_type=F32)
-                          + w1 * jnp.dot(far1, part, preferred_element_type=F32)).astype(BF16)
-        home[c].start()
+    for g in sides:
+        low = mine + 2 * g * slots
+
+        @pl.when(outer)
+        def _():
+            for c in range(chunks):
+                relay[g][c][0].wait_recv()
+
+        for c in range(chunks):
+            relay[g][c][2].wait_recv()
+        into_hidden(low, 2 * slots)
+        for c in range(chunks):
+            cut = slice(c * tile, (c + 1) * tile)
+            part = jnp.dot(hid[0:2 * slots, :], dbuf[:, cut], preferred_element_type=F32).astype(BF16)
+            outbuf[low:low + 2 * slots, cut] = part
+            farret[g, 0:slots, cut] = part[0:slots]
+
+            @pl.when(inner)
+            def _():
+                answer[g][c][1].start()
+
+            @pl.when(outer)
+            def _():
+                answer[g][c][2].start()
+                answer[g][c][3].start()
+
+    @pl.when(inner)
+    def _():
+        for g in sides:
+            unused, far0, far1 = one_hots(farid.at[g], partner, slots)
+            w0, w1 = column(farrw[g, 0:1, :]), column(farrw[g, 1:2, :])
+            for c in range(chunks):
+                cut = slice(c * tile, (c + 1) * tile)
+                for r in range(1, near):
+                    answer[g][c][r].wait_recv()
+                part = farret[g, :, cut]
+                mixfar[g, :, cut] = (w0 * jnp.dot(far0, part, preferred_element_type=F32)
+                                     + w1 * jnp.dot(far1, part, preferred_element_type=F32)).astype(BF16)
+                home[g][c].start()
 
     w0, w1 = column(rwbuf[0:1, :]), column(rwbuf[1:2, :])
     for c in back:
@@ -227,14 +276,27 @@
                            + w1 * jnp.dot(near1, part, preferred_element_type=F32))
     for c in range(chunks):
         cut = slice(c * tile, (c + 1) * tile)
-        home[c].wait_recv()
+        home[0][c].wait_recv()
         out[:, cut] = (nearsum[:, cut] + mixback[:, cut].astype(F32)).astype(BF16)
 
-    for c in meta + over + swap + direct + back + home:
+    for c in meta + over + swap + direct + back:
         c.wait_send()
-    for c in range(chunks):
-        for copy in relay[c] + farback[c]:
-            copy.wait_send()
+
+    @pl.when(inner)
+    def _():
+        for g in sides:
+            for c in range(chunks):
+                for copy in relay[g][c]:
+                    copy.wait_send()
+                answer[g][c][1].wait_send()
+                home[g][c].wait_send()
+
+    @pl.when(outer)
+    def _():
+        for g in sides:
+            for c in range(chunks):
+                answer[g][c][2].wait_send()
+                answer[g][c][3].wait_send()
 
 
 def fused(tokens, expert_ids, route_weights, gate_weight, up_weight, down_weight):
@@ -258,19 +320,21 @@
     rw_like = pltpu.VMEM((picks, toks), F32)
     sems = pltpu.SemaphoreType.DMA
     return pl.pallas_call(
-        functools.partial(kernel, chips, slots, tile),
+        functools.partial(kernel, slots, tile),
         out_shape=jax.ShapeDtypeStruct((toks, width), BF16),
         in_specs=[hbm] * 6,
         out_specs=vmem,
-        scratch_shapes=[tok_like, id_like, rw_like, tok_like, id_like, rw_like, near_like, near_like,
-                        all_like, all_like, near_like, near_like, tok_like, tok_like,
-                        pltpu.VMEM((toks, width), F32)]
+        scratch_shapes=[tok_like, id_like, rw_like,
+                        pltpu.VMEM((2, toks, width), BF16), pltpu.VMEM((2, picks, toks), jnp.int32),
+                        pltpu.VMEM((2, picks, toks), F32), near_like, pltpu.VMEM((2, mine, width), BF16),
+                        all_like, all_like, near_like, pltpu.VMEM((2, mine, width), BF16),
+                        pltpu.VMEM((2, toks, width), BF16), tok_like, pltpu.VMEM((toks, width), F32)]
         + [pltpu.VMEM((2 * half, width), BF16)] * 3
         + [pltpu.VMEM((mine, 2 * half), BF16)]
-        + [sems((6,)), sems((3,)), sems((3,)), sems((chunks,)), sems((chunks,)), sems((2,)), sems((2,)),
-           sems((near,)), sems((near,)), sems((near, chunks)), sems((near, chunks)),
-           sems((near,)), sems((near,)), sems((near, chunks)), sems((near, chunks)),
-           sems((chunks,)), sems((chunks,))],
+        + [sems((6,)), sems((3,)), sems((3,)), sems((chunks,)), sems((2, chunks)), sems((2,)), sems((2, 2)),
+           sems((near,)), sems((near,)), sems((2, near, chunks)), sems((2, 2, chunks)),
+           sems((near,)), sems((near,)), sems((2, 2, chunks)), sems((2, near, chunks)),
+           sems((2, chunks)), sems((chunks,))],
         compiler_params=pltpu.CompilerParams(
             collective_id=0, has_side_effects=True, vmem_limit_bytes=60 * 1024 * 1024),
         cost_estimate=pl.CostEstimate(
@@ -289,8 +353,7 @@
         P("wide", "narrow", None),
     )
     out_specs = P(("groups", "wide"), "narrow")
-    chips = mesh.shape["wide"] // 2
-    whole_rows = mesh.shape["narrow"] == 1 and chips >= 4 and chips & (chips - 1) == 0
+    whole_rows = mesh.shape["narrow"] == 1 and mesh.shape["wide"] == 16
     return jax.shard_map(
         fused if whole_rows else per_device, mesh=mesh, in_specs=in_specs, out_specs=out_specs, check_vma=False
     )

time: 56.8 us -> 57.9 us (1.019)
  Pallas kernels: 55 us -> 56 us
    pallas_call x1, Pallas kernels: 55 us -> 56 us  [fused(): pl.pallas_call(functools.partial(kernel, slots, tile), out_shape=jax.Shap...]
where the time goes in v5:
time: 57.9 us; the launch traced here: 57.7 us
  Pallas kernels  56 us (97%)
  local copies, waits for them, and re-layouts  1.72 us (3%)
    pallas_call x1, Pallas kernels, fused(): pl.pallas_call(functools.partial(kernel, slots, tile), out_shape=jax.Shap...  56 us
    unnamed x1, local copies, waits for them, and re-layouts  1.72 us

profile of v5, /device:TPU:0, one launch (start us, length us, event | category | flops | bytes accessed | tf_op | source)
XLA Modules:
  0.0 57.7 jit_solution(15449693980989493553)
XLA Ops:
  0.0 56.0 %shard_map.64 = bf16[64,2560]{1,0:T(8,128)(2,1)} custom-call(bf16[64,2560]{1,0:T(8,128)(2,1)} %tok.1, s32[2,64]{1,0:T(2,128)} %bitcast.2, f32[2,64]{1,0:T(2,128)} %bitcast.3, bf16[1,384,2560]{2,1,0:T(8,128)(2,1)} %gw.1, bf16[1,384,2560]{2,1,0:T(8,128)(2,1)} %uw.1, bf16[1,384,2560]{2,1,0:T(8,128)(2,1)} %dw.1), custom_call_target="tpu_custom_call" | custom-call | flops 3019898880 | bytes 6553600 | tf_op jit(solution)/shard_map/pallas_call | solution.py:322
  56.0 1.7 %copy.8 = bf16[64,2560]{1,0:T(8,128)(2,1)} copy(bf16[64,2560]{1,0:T(8,128)(2,1)} %shard_map.64) | data formatting | bytes 655360

commit v6 on v5

--- a/solution.py
+++ b/solution.py
@@ -88,8 +88,8 @@
 
 def kernel(slots, tile, tok, ids, rw, gw, uw, dw, out,
            tokbuf, idbuf, rwbuf, fartok, farid, farrw, nearsend, relaysend, recvbuf, outbuf,
-           nearret, farret, mixfar, mixback, nearsum, gbuf, ubuf, dbuf, hid,
-           local_sem, w_send, w_recv, t_send, t_recv, m_send, m_recv, n_send, n_recv,
+           nearret, farret, mixfar, mixback, nearsum, gubuf, dbuf, hid, kept, lent, lentback,
+           local_sem, s_send, s_recv, x_send, x_recv, t_send, t_recv, m_send, m_recv, n_send, n_recv,
            l_send, l_recv, b_send, b_recv, f_send, f_recv, c_send, c_recv):
     near = 4
     half = gw.shape[1]
@@ -117,14 +117,19 @@
     for to in across + [sibling] + device[1:]:
         pl.semaphore_signal(barrier, inc=1, device_id={"wide": to}, device_id_type=pl.DeviceIdType.MESH)
 
-    pairs = ((gw, gbuf), (uw, ubuf), (dw, dbuf))
-    small = [pltpu.make_async_copy(src, dst, local_sem.at[3 + i])
+    small = [pltpu.make_async_copy(src, dst, local_sem.at[1 + i])
              for i, (src, dst) in enumerate(((ids, idbuf), (rw, rwbuf), (tok, tokbuf)))]
-    local = [pltpu.make_async_copy(src.at[0], dst.at[pl.ds(0, half)], local_sem.at[i])
-             for i, (src, dst) in enumerate(pairs)]
+    lanes = 128
+    parts = half // lanes
+    local = [pltpu.make_async_copy(src.at[0, pl.ds(i * lanes, lanes)], gubuf.at[pl.ds((2 * i + p) * lanes, lanes)],
+                                   local_sem.at[4 + 2 * i + p])
+             for i in range(parts) for p, src in enumerate((gw, uw))]
+    local.append(pltpu.make_async_copy(dw.at[0], dbuf, local_sem.at[0]))
     for c in small + local:
         c.start()
 
+    sizes = [mine, 2 * slots, 2 * slots]
+    begins = [0, mine, mine + 2 * slots]
     span = [pl.ds(r * slots, slots) for r in range(2 * near)]
     cuts = [pl.ds(c * tile, tile) for c in range(chunks)]
     sides = range(2)
@@ -137,8 +142,6 @@
 
     meta, over = crossing(slot)
     arriving = [crossing(g) for g in sides]
-    swap = [remote(src.at[0], dst.at[pl.ds(half, half)], w_send.at[i], w_recv.at[i], sibling)
-            for i, (src, dst) in enumerate(pairs)]
     direct = [remote(nearsend.at[span[r]], recvbuf.at[span[r]], n_send.at[r], n_recv.at[r], device[r])
               for r in range(1, near)]
     back = [remote(outbuf.at[span[r]], nearret.at[span[r]], b_send.at[r], b_recv.at[r], device[r])
@@ -147,7 +150,15 @@
     def block(g, i):
         return span[near + 2 * g + i]
 
-    relay = [[[remote(relaysend.at[g, span[r], cuts[c]], recvbuf.at[block(g, r % 2), cuts[c]],
+    def landing(g, i):
+        return pl.ds(2 * begins[1 + g] + i * slots, slots)
+
+    share = [remote(recvbuf.at[pl.ds(2 * begins[g], sizes[g])], recvbuf.at[pl.ds(2 * begins[g] + sizes[g], sizes[g])],
+                    s_send.at[g], s_recv.at[g], sibling) for g in range(3)]
+    lend = [[remote(lent.at[pl.ds(begins[g], sizes[g]), cuts[c]], lentback.at[pl.ds(begins[g], sizes[g]), cuts[c]],
+                    x_send.at[g, c], x_recv.at[g, c], sibling) for c in range(chunks)] for g in range(3)]
+
+    relay = [[[remote(relaysend.at[g, span[r], cuts[c]], recvbuf.at[landing(g, r % 2), cuts[c]],
                       l_send.at[g, r, c], l_recv.at[g, r % 2, c], device[r]) for r in (2, 3, 1)]
               for c in range(chunks)] for g in sides]
     answer = [[[None] + [remote(outbuf.at[block(g, r % 2), cuts[c]], farret.at[g, span[r], cuts[c]],
@@ -179,9 +190,6 @@
         for c in meta + over:
             c.start()
 
-    for c in swap:
-        c.start()
-
     @pl.when(inner)
     def _():
         for g in sides:
@@ -193,42 +201,52 @@
                 arriving[g][1][c].wait_recv()
                 picked = jnp.dot(choose, fartok[g, :, cut], preferred_element_type=F32).astype(BF16)
                 relaysend[g, :, cut] = picked
-                low = mine + 2 * g * slots
+                low = 2 * begins[1 + g]
                 recvbuf[low:low + slots, cut] = picked[0:slots]
                 for copy in relay[g][c]:
                     copy.start()
 
     for c in local:
         c.wait()
-    for c in swap:
-        c.wait_recv()
-
-    hid_tile = 256
-
-    def into_hidden(base, rows):
-        @pl.loop(0, 2 * half // hid_tile)
+
+    def experts(g, answers):
+        size, base = sizes[g], 2 * begins[g]
+        share[g].start()
+        share[g].wait_recv()
+
+        @pl.loop(0, parts)
         def _(i):
-            at = pl.ds(pl.multiple_of(i * hid_tile, hid_tile), hid_tile)
-            x = recvbuf[base:base + rows, :]
-            dims = (((1,), (1,)), ((), ()))
-            gate = lax.dot_general(x, gbuf[at, :], dims, preferred_element_type=F32)
-            up = lax.dot_general(x, ubuf[at, :], dims, preferred_element_type=F32)
-            hid[0:rows, at] = (gate / (1.0 + jnp.exp(-gate)) * up).astype(BF16)
+            at = pl.ds(pl.multiple_of(i * 2 * lanes, 2 * lanes), 2 * lanes)
+            both = lax.dot_general(recvbuf[base:base + 2 * size, :], gubuf[at, :], (((1,), (1,)), ((), ())),
+                                   preferred_element_type=F32)
+            gate, up = both[:, 0:lanes], both[:, lanes:2 * lanes]
+            hid[0:2 * size, pl.ds(pl.multiple_of(i * lanes, lanes), lanes)] = (
+                gate / (1.0 + jnp.exp(-gate)) * up).astype(BF16)
+
+        low = begins[g]
+        for c in range(chunks):
+            cut = slice(c * tile, (c + 1) * tile)
+            part = jnp.dot(hid[0:2 * size, :], dbuf[:, cut], preferred_element_type=F32)
+            kept[0:size, cut] = part[0:size]
+            lent[low:low + size, cut] = part[size:2 * size].astype(BF16)
+            lend[g][c].start()
+        for c in range(chunks):
+            cut = slice(c * tile, (c + 1) * tile)
+            lend[g][c].wait_recv()
+            part = (kept[0:size, cut] + lentback[low:low + size, cut].astype(F32)).astype(BF16)
+            outbuf[low:low + size, cut] = part
+            answers(c, cut, part)
+
+    def near_answers(c, cut, part):
+        nearret[0:slots, cut] = part[0:slots]
 
     for c in direct:
         c.wait_recv()
-    into_hidden(0, mine)
-    for c in range(chunks):
-        cut = slice(c * tile, (c + 1) * tile)
-        part = jnp.dot(hid[...], dbuf[:, cut], preferred_element_type=F32).astype(BF16)
-        outbuf[0:mine, cut] = part
-        nearret[0:slots, cut] = part[0:slots]
+    experts(0, near_answers)
     for c in back:
         c.start()
 
     for g in sides:
-        low = mine + 2 * g * slots
-
         @pl.when(outer)
         def _():
             for c in range(chunks):
@@ -236,11 +254,8 @@
 
         for c in range(chunks):
             relay[g][c][2].wait_recv()
-        into_hidden(low, 2 * slots)
-        for c in range(chunks):
-            cut = slice(c * tile, (c + 1) * tile)
-            part = jnp.dot(hid[0:2 * slots, :], dbuf[:, cut], preferred_element_type=F32).astype(BF16)
-            outbuf[low:low + 2 * slots, cut] = part
+
+        def far_answers(c, cut, part):
             farret[g, 0:slots, cut] = part[0:slots]
 
             @pl.when(inner)
@@ -251,6 +266,8 @@
             def _():
                 answer[g][c][2].start()
                 answer[g][c][3].start()
+
+        experts(1 + g, far_answers)
 
     @pl.when(inner)
     def _():
@@ -279,7 +296,7 @@
         home[0][c].wait_recv()
         out[:, cut] = (nearsum[:, cut] + mixback[:, cut].astype(F32)).astype(BF16)
 
-    for c in meta + over + swap + direct + back:
+    for c in meta + over + direct + back + share + lend[0] + lend[1] + lend[2]:
         c.wait_send()
 
     @pl.when(inner)
@@ -327,11 +344,11 @@
         scratch_shapes=[tok_like, id_like, rw_like,
                         pltpu.VMEM((2, toks, width), BF16), pltpu.VMEM((2, picks, toks), jnp.int32),
                         pltpu.VMEM((2, picks, toks), F32), near_like, pltpu.VMEM((2, mine, width), BF16),
-                        all_like, all_like, near_like, pltpu.VMEM((2, mine, width), BF16),
+                        pltpu.VMEM((2 * rows, width), BF16), all_like, near_like, pltpu.VMEM((2, mine, width), BF16),
                         pltpu.VMEM((2, toks, width), BF16), tok_like, pltpu.VMEM((toks, width), F32)]
-        + [pltpu.VMEM((2 * half, width), BF16)] * 3
-        + [pltpu.VMEM((mine, 2 * half), BF16)]
-        + [sems((6,)), sems((3,)), sems((3,)), sems((chunks,)), sems((2, chunks)), sems((2,)), sems((2, 2)),
+        + [pltpu.VMEM((2 * half, width), BF16), pltpu.VMEM((half, width), BF16),
+           pltpu.VMEM((2 * mine, half), BF16), pltpu.VMEM((mine, width), F32), all_like, all_like]
+        + [sems((4 + 2 * (half // 128),)), sems((3,)), sems((3,)), sems((3, chunks)), sems((3, chunks)), sems((chunks,)), sems((2, chunks)), sems((2,)), sems((2, 2)),
            sems((near,)), sems((near,)), sems((2, near, chunks)), sems((2, 2, chunks)),
            sems((near,)), sems((near,)), sems((2, 2, chunks)), sems((2, near, chunks)),
            sems((2, chunks)), sems((chunks,))],

time: 57.9 us -> 60.2 us (1.040)
  Pallas kernels: 56 us -> 58.3 us
    pallas_call x1, Pallas kernels: 56 us -> 58.3 us  [fused(): pl.pallas_call(functools.partial(kernel, slots, tile), out_shape=jax.Shap...]
where the time goes in v6:
time: 60.2 us; the launch traced here: 60 us
  Pallas kernels  58.3 us (97%)
  local copies, waits for them, and re-layouts  1.72 us (3%)
    pallas_call x1, Pallas kernels, fused(): pl.pallas_call(functools.partial(kernel, slots, tile), out_shape=jax.Shap...  58.3 us
    unnamed x1, local copies, waits for them, and re-layouts  1.72 us

profile of v6, /device:TPU:0, one launch (start us, length us, event | category | flops | bytes accessed | tf_op | source)
XLA Modules:
  0.0 60.0 jit_solution(2148193557532466876)
XLA Ops:
  0.0 58.3 %shard_map.64 = bf16[64,2560]{1,0:T(8,128)(2,1)} custom-call(bf16[64,2560]{1,0:T(8,128)(2,1)} %tok.1, s32[2,64]{1,0:T(2,128)} %bitcast.2, f32[2,64]{1,0:T(2,128)} %bitcast.3, bf16[1,384,2560]{2,1,0:T(8,128)(2,1)} %gw.1, bf16[1,384,2560]{2,1,0:T(8,128)(2,1)} %uw.1, bf16[1,384,2560]{2,1,0:T(8,128)(2,1)} %dw.1), custom_call_target="tpu_custom_call" | custom-call | flops 3019898880 | bytes 6553600 | tf_op jit(solution)/shard_map/pallas_call | solution.py:339
  58.3 1.7 %copy.8 = bf16[64,2560]{1,0:T(8,128)(2,1)} copy(bf16[64,2560]{1,0:T(8,128)(2,1)} %shard_map.64) | data formatting | bytes 655360

commit v7 on v5

--- a/solution.py
+++ b/solution.py
@@ -88,7 +88,7 @@
 
 def kernel(slots, tile, tok, ids, rw, gw, uw, dw, out,
            tokbuf, idbuf, rwbuf, fartok, farid, farrw, nearsend, relaysend, recvbuf, outbuf,
-           nearret, farret, mixfar, mixback, nearsum, gbuf, ubuf, dbuf, hid,
+           nearret, farret, mixfar, mixback, nearsum, gbuf, ubuf, dbuf, hid, turned,
            local_sem, w_send, w_recv, t_send, t_recv, m_send, m_recv, n_send, n_recv,
            l_send, l_recv, b_send, b_recv, f_send, f_recv, c_send, c_recv):
     near = 4
@@ -205,19 +205,24 @@
 
     hid_tile = 256
 
-    def into_hidden(base, rows):
+    def turn(base, rows, c):
+        cut = slice(c * tile, (c + 1) * tile)
+        turned[cut, 0:rows] = jnp.transpose(recvbuf[base:base + rows, cut])
+
+    def into_hidden(rows):
         @pl.loop(0, 2 * half // hid_tile)
         def _(i):
             at = pl.ds(pl.multiple_of(i * hid_tile, hid_tile), hid_tile)
-            x = recvbuf[base:base + rows, :]
-            dims = (((1,), (1,)), ((), ()))
-            gate = lax.dot_general(x, gbuf[at, :], dims, preferred_element_type=F32)
-            up = lax.dot_general(x, ubuf[at, :], dims, preferred_element_type=F32)
-            hid[0:rows, at] = (gate / (1.0 + jnp.exp(-gate)) * up).astype(BF16)
+            x = turned[:, 0:rows]
+            gate = jnp.dot(gbuf[at, :], x, preferred_element_type=F32)
+            up = jnp.dot(ubuf[at, :], x, preferred_element_type=F32)
+            hid[0:rows, at] = jnp.transpose(gate / (1.0 + jnp.exp(-gate)) * up).astype(BF16)
 
     for c in direct:
         c.wait_recv()
-    into_hidden(0, mine)
+    for c in range(chunks):
+        turn(0, mine, c)
+    into_hidden(mine)
     for c in range(chunks):
         cut = slice(c * tile, (c + 1) * tile)
         part = jnp.dot(hid[...], dbuf[:, cut], preferred_element_type=F32).astype(BF16)
@@ -229,14 +234,14 @@
     for g in sides:
         low = mine + 2 * g * slots
 
-        @pl.when(outer)
-        def _():
-            for c in range(chunks):
+        for c in range(chunks):
+            @pl.when(outer)
+            def _():
                 relay[g][c][0].wait_recv()
 
-        for c in range(chunks):
             relay[g][c][2].wait_recv()
-        into_hidden(low, 2 * slots)
+            turn(low, 2 * slots, c)
+        into_hidden(2 * slots)
         for c in range(chunks):
             cut = slice(c * tile, (c + 1) * tile)
             part = jnp.dot(hid[0:2 * slots, :], dbuf[:, cut], preferred_element_type=F32).astype(BF16)
@@ -330,7 +335,7 @@
                         all_like, all_like, near_like, pltpu.VMEM((2, mine, width), BF16),
                         pltpu.VMEM((2, toks, width), BF16), tok_like, pltpu.VMEM((toks, width), F32)]
         + [pltpu.VMEM((2 * half, width), BF16)] * 3
-        + [pltpu.VMEM((mine, 2 * half), BF16)]
+        + [pltpu.VMEM((mine, 2 * half), BF16), pltpu.VMEM((width, mine), BF16)]
         + [sems((6,)), sems((3,)), sems((3,)), sems((chunks,)), sems((2, chunks)), sems((2,)), sems((2, 2)),
            sems((near,)), sems((near,)), sems((2, near, chunks)), sems((2, 2, chunks)),
            sems((near,)), sems((near,)), sems((2, 2, chunks)), sems((2, near, chunks)),

time: 57.9 us -> 57.9 us (level)
  no operation moved by 1% of the time
where the time goes in v7:
time: 57.9 us; the launch traced here: 57.7 us
  Pallas kernels  56 us (97%)
  local copies, waits for them, and re-layouts  1.72 us (3%)
    pallas_call x1, Pallas kernels, fused(): pl.pallas_call(functools.partial(kernel, slots, tile), out_shape=jax.Shap...  56 us
    unnamed x1, local copies, waits for them, and re-layouts  1.72 us

profile of v7, /device:TPU:0, one launch (start us, length us, event | category | flops | bytes accessed | tf_op | source)
XLA Modules:
  0.0 57.7 jit_solution(11325481719854750685)
XLA Ops:
  0.0 56.0 %shard_map.64 = bf16[64,2560]{1,0:T(8,128)(2,1)} custom-call(bf16[64,2560]{1,0:T(8,128)(2,1)} %tok.1, s32[2,64]{1,0:T(2,128)} %bitcast.2, f32[2,64]{1,0:T(2,128)} %bitcast.3, bf16[1,384,2560]{2,1,0:T(8,128)(2,1)} %gw.1, bf16[1,384,2560]{2,1,0:T(8,128)(2,1)} %uw.1, bf16[1,384,2560]{2,1,0:T(8,128)(2,1)} %dw.1), custom_call_target="tpu_custom_call" | custom-call | flops 3019898880 | bytes 6553600 | tf_op jit(solution)/shard_map/pallas_call | solution.py:327
  56.0 1.7 %copy.8 = bf16[64,2560]{1,0:T(8,128)(2,1)} copy(bf16[64,2560]{1,0:T(8,128)(2,1)} %shard_map.64) | data formatting | bytes 655360

commit v8 on v5

--- a/solution.py
+++ b/solution.py
@@ -215,18 +215,19 @@
             up = lax.dot_general(x, ubuf[at, :], dims, preferred_element_type=F32)
             hid[0:rows, at] = (gate / (1.0 + jnp.exp(-gate)) * up).astype(BF16)
 
-    for c in direct:
-        c.wait_recv()
-    into_hidden(0, mine)
-    for c in range(chunks):
-        cut = slice(c * tile, (c + 1) * tile)
-        part = jnp.dot(hid[...], dbuf[:, cut], preferred_element_type=F32).astype(BF16)
-        outbuf[0:mine, cut] = part
-        nearret[0:slots, cut] = part[0:slots]
-    for c in back:
-        c.start()
-
-    for g in sides:
+    def near_group():
+        for c in direct:
+            c.wait_recv()
+        into_hidden(0, mine)
+        for c in range(chunks):
+            cut = slice(c * tile, (c + 1) * tile)
+            part = jnp.dot(hid[...], dbuf[:, cut], preferred_element_type=F32).astype(BF16)
+            outbuf[0:mine, cut] = part
+            nearret[0:slots, cut] = part[0:slots]
+        for c in back:
+            c.start()
+
+    def relayed_group(g):
         low = mine + 2 * g * slots
 
         @pl.when(outer)
@@ -252,9 +253,9 @@
                 answer[g][c][2].start()
                 answer[g][c][3].start()
 
-    @pl.when(inner)
-    def _():
-        for g in sides:
+    def send_home(g):
+        @pl.when(inner)
+        def _():
             unused, far0, far1 = one_hots(farid.at[g], partner, slots)
             w0, w1 = column(farrw[g, 0:1, :]), column(farrw[g, 1:2, :])
             for c in range(chunks):
@@ -265,6 +266,12 @@
                 mixfar[g, :, cut] = (w0 * jnp.dot(far0, part, preferred_element_type=F32)
                                      + w1 * jnp.dot(far1, part, preferred_element_type=F32)).astype(BF16)
                 home[g][c].start()
+
+    relayed_group(0)
+    near_group()
+    send_home(0)
+    relayed_group(1)
+    send_home(1)
 
     w0, w1 = column(rwbuf[0:1, :]), column(rwbuf[1:2, :])
     for c in back:
@@ -336,7 +343,7 @@
            sems((near,)), sems((near,)), sems((2, 2, chunks)), sems((2, near, chunks)),
            sems((2, chunks)), sems((chunks,))],
         compiler_params=pltpu.CompilerParams(
-            collective_id=0, has_side_effects=True, vmem_limit_bytes=60 * 1024 * 1024),
+            collective_id=0, has_side_effects=True, vmem_limit_bytes=(53 * 1024 + 512) * 1024),
         cost_estimate=pl.CostEstimate(
             flops=12 * rows * half * width, bytes_accessed=6 * half * width + 4 * toks * width,
             transcendentals=2 * rows * half),

time: 57.9 us -> 55.5 us (0.959)
  Pallas kernels: 56 us -> 53.2 us
    pallas_call x1, Pallas kernels: 56 us -> 53.2 us  [fused(): pl.pallas_call(functools.partial(kernel, slots, tile), out_shape=jax.Shap...]
    unnamed x1 -> x5, local copies, waits for them, and re-layouts: 1.72 us -> 2.08 us
where the time goes in v8:
time: 55.5 us; the launch traced here: 55.3 us
  Pallas kernels  53.2 us (96%)
  local copies, waits for them, and re-layouts  2.08 us (4%)
    pallas_call x1, Pallas kernels, fused(): pl.pallas_call(functools.partial(kernel, slots, tile), out_shape=jax.Shap...  53.2 us
    unnamed x5, local copies, waits for them, and re-layouts  2.08 us

profile of v8, /device:TPU:0, one launch (start us, length us, event | category | flops | bytes accessed | tf_op | source)
XLA Modules:
  0.0 55.3 jit_solution(16984416086490831029)
XLA Ops:
  0.0 0.0 copy-start
  0.0 0.7 %copy-done = s32[64,2]{0,1:T(2,128)S(1)} copy-done((s32[64,2]{0,1:T(2,128)S(1)}, s32[64,2]{0,1:T(2,128)}, u32[]{:S(2)}) %copy-start) | copy-done | bytes 536
  0.7 0.0 copy-start.1
  0.7 0.7 %copy-done.1 = f32[64,2]{0,1:T(2,128)S(1)} copy-done((f32[64,2]{0,1:T(2,128)S(1)}, f32[64,2]{0,1:T(2,128)}, u32[]{:S(2)}) %copy-start.1) | copy-done | bytes 536
  1.4 53.2 %shard_map.64 = bf16[64,2560]{1,0:T(8,128)(2,1)S(1)} custom-call(bf16[64,2560]{1,0:T(8,128)(2,1)} %tok.1, s32[2,64]{1,0:T(2,128)S(1)} %bitcast.2, f32[2,64]{1,0:T(2,128)S(1)} %bitcast.3, bf16[1,384,2560]{2,1,0:T(8,128)(2,1)} %gw.1, bf16[1,384,2560]{2,1,0:T(8,128)(2,1)} %uw.1, bf16[1,384,2560]{2,1,0:T(8,128)(2,1)} %dw.1), custom_call_target="tpu_custom_call" | custom-call | flops 3019898880 | bytes 6553600 | tf_op jit(solution)/shard_map/pallas_call | solution.py:329
  54.6 0.7 %copy.8 = bf16[64,2560]{1,0:T(8,128)(2,1)} copy(bf16[64,2560]{1,0:T(8,128)(2,1)S(1)} %shard_map.64) | data formatting | bytes 655360
Async XLA Ops:
  0.0 0.7 %copy-start = (s32[64,2]{0,1:T(2,128)S(1)}, s32[64,2]{0,1:T(2,128)}, u32[]{:S(2)}) copy-start(s32[64,2]{0,1:T(2,128)} %param.7) | copy-start | bytes 1540
  0.7 0.7 %copy-start.1 = (f32[64,2]{0,1:T(2,128)S(1)}, f32[64,2]{0,1:T(2,128)}, u32[]{:S(2)}) copy-start(f32[64,2]{0,1:T(2,128)} %param.8) | copy-start | bytes 1540

commit v9 on v8

--- a/solution.py
+++ b/solution.py
@@ -267,8 +267,8 @@
                                      + w1 * jnp.dot(far1, part, preferred_element_type=F32)).astype(BF16)
                 home[g][c].start()
 
+    near_group()
     relayed_group(0)
-    near_group()
     send_home(0)
     relayed_group(1)
     send_home(1)

time: 55.5 us -> 60 us (1.081)
  Pallas kernels: 53.2 us -> 57.7 us
    pallas_call x1, Pallas kernels: 53.2 us -> 57.7 us  [fused(): pl.pallas_call(functools.partial(kernel, slots, tile), out_shape=jax.Shap...]
where the time goes in v9:
time: 60 us; the launch traced here: 59.8 us
  Pallas kernels  57.7 us (96%)
  local copies, waits for them, and re-layouts  2.08 us (3%)
    pallas_call x1, Pallas kernels, fused(): pl.pallas_call(functools.partial(kernel, slots, tile), out_shape=jax.Shap...  57.7 us
    unnamed x5, local copies, waits for them, and re-layouts  2.08 us

profile of v9, /device:TPU:0, one launch (start us, length us, event | category | flops | bytes accessed | tf_op | source)
XLA Modules:
  0.0 59.8 jit_solution(11634418656770084780)
XLA Ops:
  0.0 0.0 copy-start
  0.0 0.7 %copy-done = s32[64,2]{0,1:T(2,128)S(1)} copy-done((s32[64,2]{0,1:T(2,128)S(1)}, s32[64,2]{0,1:T(2,128)}, u32[]{:S(2)}) %copy-start) | copy-done | bytes 536
  0.7 0.0 copy-start.1
  0.7 0.7 %copy-done.1 = f32[64,2]{0,1:T(2,128)S(1)} copy-done((f32[64,2]{0,1:T(2,128)S(1)}, f32[64,2]{0,1:T(2,128)}, u32[]{:S(2)}) %copy-start.1) | copy-done | bytes 536
  1.4 57.7 %shard_map.64 = bf16[64,2560]{1,0:T(8,128)(2,1)S(1)} custom-call(bf16[64,2560]{1,0:T(8,128)(2,1)} %tok.1, s32[2,64]{1,0:T(2,128)S(1)} %bitcast.2, f32[2,64]{1,0:T(2,128)S(1)} %bitcast.3, bf16[1,384,2560]{2,1,0:T(8,128)(2,1)} %gw.1, bf16[1,384,2560]{2,1,0:T(8,128)(2,1)} %uw.1, bf16[1,384,2560]{2,1,0:T(8,128)(2,1)} %dw.1), custom_call_target="tpu_custom_call" | custom-call | flops 3019898880 | bytes 6553600 | tf_op jit(solution)/shard_map/pallas_call | solution.py:329
  59.1 0.7 %copy.8 = bf16[64,2560]{1,0:T(8,128)(2,1)} copy(bf16[64,2560]{1,0:T(8,128)(2,1)S(1)} %shard_map.64) | data formatting | bytes 655360
Async XLA Ops:
  0.0 0.7 %copy-start = (s32[64,2]{0,1:T(2,128)S(1)}, s32[64,2]{0,1:T(2,128)}, u32[]{:S(2)}) copy-start(s32[64,2]{0,1:T(2,128)} %param.7) | copy-start | bytes 1540
  0.7 0.7 %copy-start.1 = (f32[64,2]{0,1:T(2,128)S(1)}, f32[64,2]{0,1:T(2,128)}, u32[]{:S(2)}) copy-start(f32[64,2]{0,1:T(2,128)} %param.8) | copy-start | bytes 1540

commit v10 on v9

--- a/solution.py
+++ b/solution.py
@@ -215,34 +215,23 @@
             up = lax.dot_general(x, ubuf[at, :], dims, preferred_element_type=F32)
             hid[0:rows, at] = (gate / (1.0 + jnp.exp(-gate)) * up).astype(BF16)
 
-    def near_group():
-        for c in direct:
-            c.wait_recv()
-        into_hidden(0, mine)
+    def group(low, rows, g):
+        @pl.when(outer)
+        def _():
+            for c in range(chunks):
+                relay[g][c][0].wait_recv()
+
+        for c in range(chunks):
+            relay[g][c][2].wait_recv()
+        into_hidden(low, rows)
+        at = rows - 2 * slots
         for c in range(chunks):
             cut = slice(c * tile, (c + 1) * tile)
-            part = jnp.dot(hid[...], dbuf[:, cut], preferred_element_type=F32).astype(BF16)
-            outbuf[0:mine, cut] = part
-            nearret[0:slots, cut] = part[0:slots]
-        for c in back:
-            c.start()
-
-    def relayed_group(g):
-        low = mine + 2 * g * slots
-
-        @pl.when(outer)
-        def _():
-            for c in range(chunks):
-                relay[g][c][0].wait_recv()
-
-        for c in range(chunks):
-            relay[g][c][2].wait_recv()
-        into_hidden(low, 2 * slots)
-        for c in range(chunks):
-            cut = slice(c * tile, (c + 1) * tile)
-            part = jnp.dot(hid[0:2 * slots, :], dbuf[:, cut], preferred_element_type=F32).astype(BF16)
-            outbuf[low:low + 2 * slots, cut] = part
-            farret[g, 0:slots, cut] = part[0:slots]
+            part = jnp.dot(hid[0:rows, :], dbuf[:, cut], preferred_element_type=F32).astype(BF16)
+            outbuf[low:low + rows, cut] = part
+            farret[g, 0:slots, cut] = part[at:at + slots]
+            if g == 0:
+                nearret[0:slots, cut] = part[0:slots]
 
             @pl.when(inner)
             def _():
@@ -267,10 +256,13 @@
                                      + w1 * jnp.dot(far1, part, preferred_element_type=F32)).astype(BF16)
                 home[g][c].start()
 
-    near_group()
-    relayed_group(0)
+    for c in direct:
+        c.wait_recv()
+    group(0, mine + 2 * slots, 0)
+    for c in back:
+        c.start()
     send_home(0)
-    relayed_group(1)
+    group(mine + 2 * slots, 2 * slots, 1)
     send_home(1)
 
     w0, w1 = column(rwbuf[0:1, :]), column(rwbuf[1:2, :])
@@ -337,7 +329,7 @@
                         all_like, all_like, near_like, pltpu.VMEM((2, mine, width), BF16),
                         pltpu.VMEM((2, toks, width), BF16), tok_like, pltpu.VMEM((toks, width), F32)]
         + [pltpu.VMEM((2 * half, width), BF16)] * 3
-        + [pltpu.VMEM((mine, 2 * half), BF16)]
+        + [pltpu.VMEM((mine + 2 * slots, 2 * half), BF16)]
         + [sems((6,)), sems((3,)), sems((3,)), sems((chunks,)), sems((2, chunks)), sems((2,)), sems((2, 2)),
            sems((near,)), sems((near,)), sems((2, near, chunks)), sems((2, 2, chunks)),
            sems((near,)), sems((near,)), sems((2, 2, chunks)), sems((2, near, chunks)),

time: 60 us -> 55.7 us (0.928)
  Pallas kernels: 57.7 us -> 53.4 us
    pallas_call x1, Pallas kernels: 57.7 us -> 53.4 us  [fused(): pl.pallas_call(functools.partial(kernel, slots, tile), out_shape=jax.Shap...]
where the time goes in v10:
time: 55.7 us; the launch traced here: 55.5 us
  Pallas kernels  53.4 us (96%)
  local copies, waits for them, and re-layouts  2.08 us (4%)
    pallas_call x1, Pallas kernels, fused(): pl.pallas_call(functools.partial(kernel, slots, tile), out_shape=jax.Shap...  53.4 us
    unnamed x5, local copies, waits for them, and re-layouts  2.08 us

profile of v10, /device:TPU:0, one launch (start us, length us, event | category | flops | bytes accessed | tf_op | source)
XLA Modules:
  0.0 55.5 jit_solution(11639043286382942378)
XLA Ops:
  0.0 0.0 copy-start
  0.0 0.7 %copy-done = s32[64,2]{0,1:T(2,128)S(1)} copy-done((s32[64,2]{0,1:T(2,128)S(1)}, s32[64,2]{0,1:T(2,128)}, u32[]{:S(2)}) %copy-start) | copy-done | bytes 536
  0.7 0.0 copy-start.1
  0.7 0.7 %copy-done.1 = f32[64,2]{0,1:T(2,128)S(1)} copy-done((f32[64,2]{0,1:T(2,128)S(1)}, f32[64,2]{0,1:T(2,128)}, u32[]{:S(2)}) %copy-start.1) | copy-done | bytes 536
  1.4 53.4 %shard_map.64 = bf16[64,2560]{1,0:T(8,128)(2,1)S(1)} custom-call(bf16[64,2560]{1,0:T(8,128)(2,1)} %tok.1, s32[2,64]{1,0:T(2,128)S(1)} %bitcast.2, f32[2,64]{1,0:T(2,128)S(1)} %bitcast.3, bf16[1,384,2560]{2,1,0:T(8,128)(2,1)} %gw.1, bf16[1,384,2560]{2,1,0:T(8,128)(2,1)} %uw.1, bf16[1,384,2560]{2,1,0:T(8,128)(2,1)} %dw.1), custom_call_target="tpu_custom_call" | custom-call | flops 3019898880 | bytes 6553600 | tf_op jit(solution)/shard_map/pallas_call | solution.py:321
  54.8 0.7 %copy.8 = bf16[64,2560]{1,0:T(8,128)(2,1)} copy(bf16[64,2560]{1,0:T(8,128)(2,1)S(1)} %shard_map.64) | data formatting | bytes 655360
Async XLA Ops:
  0.0 0.7 %copy-start = (s32[64,2]{0,1:T(2,128)S(1)}, s32[64,2]{0,1:T(2,128)}, u32[]{:S(2)}) copy-start(s32[64,2]{0,1:T(2,128)} %param.7) | copy-start | bytes 1540
  0.7 0.7 %copy-start.1 = (f32[64,2]{0,1:T(2,128)S(1)}, f32[64,2]{0,1:T(2,128)}, u32[]{:S(2)}) copy-start(f32[64,2]{0,1:T(2,128)} %param.8) | copy-start | bytes 1540

commit v11 on v8

--- a/solution.py
+++ b/solution.py
@@ -158,10 +158,8 @@
 
     pl.semaphore_wait(barrier, near + 2)
 
-    @pl.when(inner)
-    def _():
-        for c in meta + over:
-            c.start()
+    for c in meta + over:
+        c.start()
 
     for c in small:
         c.wait()
@@ -173,11 +171,6 @@
         recvbuf[0:slots, cut] = picked[0:slots]
     for c in direct:
         c.start()
-
-    @pl.when(outer)
-    def _():
-        for c in meta + over:
-            c.start()
 
     for c in swap:
         c.start()

time: 55.5 us -> 57.5 us (1.036)
  Pallas kernels: 53.2 us -> 55.2 us
    pallas_call x1, Pallas kernels: 53.2 us -> 55.2 us  [fused(): pl.pallas_call(functools.partial(kernel, slots, tile), out_shape=jax.Shap...]
where the time goes in v11:
time: 57.5 us; the launch traced here: 57.3 us
  Pallas kernels  55.2 us (96%)
  local copies, waits for them, and re-layouts  2.08 us (4%)
    pallas_call x1, Pallas kernels, fused(): pl.pallas_call(functools.partial(kernel, slots, tile), out_shape=jax.Shap...  55.2 us
    unnamed x5, local copies, waits for them, and re-layouts  2.08 us

profile of v11, /device:TPU:0, one launch (start us, length us, event | category | flops | bytes accessed | tf_op | source)
XLA Modules:
  0.0 57.3 jit_solution(8823012206744317042)
XLA Ops:
  0.0 0.0 copy-start
  0.0 0.7 %copy-done = s32[64,2]{0,1:T(2,128)S(1)} copy-done((s32[64,2]{0,1:T(2,128)S(1)}, s32[64,2]{0,1:T(2,128)}, u32[]{:S(2)}) %copy-start) | copy-done | bytes 536
  0.7 0.0 copy-start.1
  0.7 0.7 %copy-done.1 = f32[64,2]{0,1:T(2,128)S(1)} copy-done((f32[64,2]{0,1:T(2,128)S(1)}, f32[64,2]{0,1:T(2,128)}, u32[]{:S(2)}) %copy-start.1) | copy-done | bytes 536
  1.4 55.2 %shard_map.64 = bf16[64,2560]{1,0:T(8,128)(2,1)S(1)} custom-call(bf16[64,2560]{1,0:T(8,128)(2,1)} %tok.1, s32[2,64]{1,0:T(2,128)S(1)} %bitcast.2, f32[2,64]{1,0:T(2,128)S(1)} %bitcast.3, bf16[1,384,2560]{2,1,0:T(8,128)(2,1)} %gw.1, bf16[1,384,2560]{2,1,0:T(8,128)(2,1)} %uw.1, bf16[1,384,2560]{2,1,0:T(8,128)(2,1)} %dw.1), custom_call_target="tpu_custom_call" | custom-call | flops 3019898880 | bytes 6553600 | tf_op jit(solution)/shard_map/pallas_call | solution.py:322
  56.6 0.7 %copy.8 = bf16[64,2560]{1,0:T(8,128)(2,1)} copy(bf16[64,2560]{1,0:T(8,128)(2,1)S(1)} %shard_map.64) | data formatting | bytes 655360
Async XLA Ops:
  0.0 0.7 %copy-start = (s32[64,2]{0,1:T(2,128)S(1)}, s32[64,2]{0,1:T(2,128)}, u32[]{:S(2)}) copy-start(s32[64,2]{0,1:T(2,128)} %param.7) | copy-start | bytes 1540
  0.7 0.7 %copy-start.1 = (f32[64,2]{0,1:T(2,128)S(1)}, f32[64,2]{0,1:T(2,128)}, u32[]{:S(2)}) copy-start(f32[64,2]{0,1:T(2,128)} %param.8) | copy-start | bytes 1540
